TPU v7x, 32 devices: a whole 2x2x4 slice. The times are simulated.
32 devices in a mesh: dp: 4 (over z), row: 4 (over x, core), col: 2 (over y).
Axes of the slice: x: 2, y: 2, z: 4, core: 2. Of those that a mesh axis runs over, the one named last changes fastest.
Arguments:
- tokens: bfloat16 [32768, 1024], P(('dp', 'row'), 'col'), may hold values from -6 to 6
- segment_ids: int32 [32768], P('dp'), may hold values from 0 to 3, as said below
- norm_one: float32 [1024], P('col'), may hold values from 0.3 to 4.6
- qkv_weight: bfloat16 [1024, 3, 16, 64], P('col', None, 'row'), may hold values from -0.1875 to 0.1875
- attn_out_weight: bfloat16 [1024, 1024], P('row', 'col'), may hold values from -0.75 to 0.75
- norm_two: float32 [1024], P('col'), may hold values from 0.3 to 4.6
- in_weight: bfloat16 [1024, 2, 2624], P('col', None, 'row'), may hold values from -0.1875 to 0.1875
- out_weight: bfloat16 [2624, 1024], P('row', 'col'), may hold values from -0.125 to 0.125
- cotangent: bfloat16 [32768, 1024], P(('dp', 'row'), 'col'), may hold values from -6 to 6
Outputs:
- result: bfloat16 [32768, 1024], P(('dp', 'row'), 'col')
- grad_tokens: float32 [32768, 1024], P(('dp', 'row'), 'col')
- grad_norm_one: float32 [1024], P('col')
- grad_qkv: float32 [1024, 3, 16, 64], P('col', None, 'row')
- grad_attn_out: float32 [1024, 1024], P('row', 'col')
- grad_norm_two: float32 [1024], P('col')
- grad_in: float32 [1024, 2, 2624], P('col', None, 'row')
- grad_out: float32 [2624, 1024], P('row', 'col')
Inputs may be any that keep to these rules, and one draw needn't show every extreme that they name: `segment_ids`: each sequence of 4096 tokens (aligned blocks of the array) holds 4 documents numbered from 0 in order, each of 200 tokens or more, one of exactly 2000 tokens.
All inputs are finite; a program needn't handle non-finite values.
Results may differ from a plain program's by a relative error of at most 0.018.
Values may be sent and summed in bfloat16 or wider, within the bound.
A program may use at most 256 MiB of HBM per device.

v0:
```python
import jax
import jax.numpy as jnp
from jax import lax
from jax.sharding import PartitionSpec as P

WINDOW = 128
SEQ = 4096


EPS = 1e-05
NEG = -1e30
THETA = 10000.0


def norm_forward(inputs, gain_vec):
    width = lax.axis_size("col") * inputs.shape[1]
    sum_rows, square_rows = lax.psum((jnp.sum(inputs, 1), jnp.sum(inputs * inputs, 1)), "col")
    average = sum_rows / width
    variance = square_rows / width - average * average
    inverse_std = lax.rsqrt(variance + EPS)
    unit_rows = (inputs - average[:, None]) * inverse_std[:, None]
    return (unit_rows * gain_vec, unit_rows, inverse_std)


def norm_backward(grad_normed, unit_rows, inverse_std, gain_vec):
    width = lax.axis_size("col") * grad_normed.shape[1]
    scaled = grad_normed * gain_vec
    sum_rows, cross_rows = lax.psum((jnp.sum(scaled, 1), jnp.sum(scaled * unit_rows, 1)), "col")
    grad_inputs = inverse_std[:, None] * (
        scaled - sum_rows[:, None] / width - unit_rows * (cross_rows[:, None] / width)
    )
    return (grad_inputs, jnp.sum(grad_normed * unit_rows, 0))


def contract_rows(left, right):
    return lax.dot_general(
        left, right, (((0,), (0,)), ((), ())), preferred_element_type=jnp.float32
    )


def contract_cols(left, right):
    return lax.dot_general(
        left, right, (((1,), (1,)), ((), ())), preferred_element_type=jnp.float32
    )


def project_in(normed_low, weight_flat):
    gathered = lax.all_gather(normed_low, "row", axis=0, tiled=True)
    product = lax.psum_scatter(
        jnp.dot(gathered, weight_flat, preferred_element_type=jnp.float32),
        "col",
        scatter_dimension=0,
        tiled=True,
    )
    return (gathered, product)


def project_out(acts_low, weight):
    gathered = lax.all_gather(acts_low, "col", axis=0, tiled=True)
    product = lax.psum_scatter(
        jnp.dot(gathered, weight, preferred_element_type=jnp.float32),
        "row",
        scatter_dimension=0,
        tiled=True,
    )
    return (gathered, product)


def back_out(grad_low, kept, weight):
    gathered = lax.all_gather(grad_low, "row", axis=0, tiled=True)
    grad_weight = contract_rows(kept, gathered)
    grad_acts = lax.psum_scatter(
        contract_cols(gathered, weight), "col", scatter_dimension=0, tiled=True
    )
    return (grad_acts, grad_weight)


def back_in(grad_low, kept, weight_flat):
    gathered = lax.all_gather(grad_low, "col", axis=0, tiled=True)
    grad_weight = contract_rows(kept, gathered)
    grad_normed = lax.psum_scatter(
        contract_cols(gathered, weight_flat), "row", scatter_dimension=0, tiled=True
    )
    return (grad_normed, grad_weight)


def rotary_tables(length, head_size):
    frequencies = THETA ** (-jnp.arange(head_size // 2, dtype=jnp.float32) * 2.0 / head_size)
    angles = jnp.arange(length, dtype=jnp.float32)[:, None] * frequencies[None, :]
    angles = jnp.concatenate([angles, angles], -1)
    return (jnp.cos(angles), jnp.sin(angles))


def rotate(values_in, cos_tab, sin_tab):
    half_size = values_in.shape[-1] // 2
    turned = jnp.concatenate([-values_in[..., half_size:], values_in[..., :half_size]], -1)
    return values_in * cos_tab[:, None, :] + turned * sin_tab[:, None, :]


def block_parts(offset, query_seq, key_pad, value_pad, seg_pad, block_len, half_win):
    key_span = block_len + 2 * half_win
    query_blk = lax.dynamic_slice_in_dim(query_seq, offset, block_len, 0)
    key_blk = lax.dynamic_slice_in_dim(key_pad, offset, key_span, 0)
    value_blk = lax.dynamic_slice_in_dim(value_pad, offset, key_span, 0)
    seg_query = lax.dynamic_slice_in_dim(seg_pad, offset + half_win, block_len, 0)
    seg_key = lax.dynamic_slice_in_dim(seg_pad, offset, key_span, 0)
    distance = (
        lax.broadcasted_iota(jnp.int32, (block_len, key_span), 1)
        - lax.broadcasted_iota(jnp.int32, (block_len, key_span), 0)
        - half_win
    )
    allowed = (seg_query[:, None] == seg_key[None, :]) & (jnp.abs(distance) <= half_win)
    return (query_blk, key_blk, value_blk, allowed)


def block_scores(query_blk, key_blk, allowed, scaling):
    scores = (
        jnp.einsum("qhd,khd->hqk", query_blk, key_blk, preferred_element_type=jnp.float32) * scaling
    )
    return jnp.where(allowed[None], scores, NEG)


def padded_inputs(key_seq, value_seq, seg_seq, half_win):
    pad_spec = ((half_win, half_win), (0, 0), (0, 0))
    seg_pad = jnp.pad(seg_seq, (half_win, half_win), constant_values=-1)
    return (jnp.pad(key_seq, pad_spec), jnp.pad(value_seq, pad_spec), seg_pad)


def attend_sequence(query_seq, key_seq, value_seq, seg_seq):
    half_win = WINDOW // 2
    block_len = min(512, SEQ)
    key_pad, value_pad, seg_pad = padded_inputs(key_seq, value_seq, seg_seq, half_win)
    scaling = query_seq.shape[2] ** (-0.5)

    def one_block(offset):
        query_blk, key_blk, value_blk, allowed = block_parts(
            offset, query_seq, key_pad, value_pad, seg_pad, block_len, half_win
        )
        scores = block_scores(query_blk, key_blk, allowed, scaling)
        highest = jnp.max(scores, -1, keepdims=True)
        weights = jnp.exp(scores - highest)
        totals = jnp.sum(weights, -1, keepdims=True)
        attn_probs = (weights / totals).astype(jnp.bfloat16)
        mixture = jnp.einsum(
            "hqk,khd->qhd", attn_probs, value_blk, preferred_element_type=jnp.float32
        )
        return (mixture.astype(jnp.bfloat16), (highest + jnp.log(totals))[..., 0])

    offsets = jnp.arange(SEQ // block_len, dtype=jnp.int32) * block_len
    mixture, log_totals = lax.map(one_block, offsets)
    return (mixture.reshape(query_seq.shape), log_totals)


def attend_back_sequence(query_seq, key_seq, value_seq, seg_seq, log_totals, grad_seq):
    half_win = WINDOW // 2
    block_len = min(512, SEQ)
    key_span = block_len + 2 * half_win
    key_pad, value_pad, seg_pad = padded_inputs(key_seq, value_seq, seg_seq, half_win)
    scaling = query_seq.shape[2] ** (-0.5)

    def one_block(carried, scan_item):
        offset, log_blk = scan_item
        query_blk, key_blk, value_blk, allowed = block_parts(
            offset, query_seq, key_pad, value_pad, seg_pad, block_len, half_win
        )
        scores = block_scores(query_blk, key_blk, allowed, scaling)
        attn_probs = jnp.exp(scores - log_blk[..., None])
        grad_blk = lax.dynamic_slice_in_dim(grad_seq, offset, block_len, 0)
        grad_probs = jnp.einsum(
            "qhd,khd->hqk", grad_blk, value_blk, preferred_element_type=jnp.float32
        )
        grad_values = jnp.einsum(
            "hqk,qhd->khd",
            attn_probs.astype(jnp.bfloat16),
            grad_blk,
            preferred_element_type=jnp.float32,
        )
        centre = jnp.sum(grad_probs * attn_probs, -1, keepdims=True)
        grad_scores = (attn_probs * (grad_probs - centre)).astype(jnp.bfloat16)
        grad_queries = (
            jnp.einsum("hqk,khd->qhd", grad_scores, key_blk, preferred_element_type=jnp.float32)
            * scaling
        )
        grad_keys = (
            jnp.einsum("hqk,qhd->khd", grad_scores, query_blk, preferred_element_type=jnp.float32)
            * scaling
        )
        key_acc, value_acc = carried
        key_acc = lax.dynamic_update_slice_in_dim(
            key_acc, lax.dynamic_slice_in_dim(key_acc, offset, key_span, 0) + grad_keys, offset, 0
        )
        value_acc = lax.dynamic_update_slice_in_dim(
            value_acc,
            lax.dynamic_slice_in_dim(value_acc, offset, key_span, 0) + grad_values,
            offset,
            0,
        )
        return ((key_acc, value_acc), grad_queries)

    offsets = jnp.arange(SEQ // block_len, dtype=jnp.int32) * block_len
    zeros_pad = jnp.zeros(key_pad.shape, jnp.float32)
    (key_acc, value_acc), grad_queries = lax.scan(
        one_block, (zeros_pad, zeros_pad), (offsets, log_totals)
    )
    return (
        grad_queries.reshape(query_seq.shape),
        key_acc[half_win : half_win + SEQ],
        value_acc[half_win : half_win + SEQ],
    )


def by_sequence(array_in):
    return array_in.reshape((array_in.shape[0] // SEQ, SEQ) + array_in.shape[1:])


def attend_all(queries, key_vecs, values, segments):

    def per_sequence(parts_in):
        return attend_sequence(parts_in[0], parts_in[1], parts_in[2], parts_in[3])

    mixture, log_totals = lax.map(
        per_sequence,
        (by_sequence(queries), by_sequence(key_vecs), by_sequence(values), by_sequence(segments)),
    )
    return (mixture.reshape(queries.shape), log_totals)


def attend_back_all(queries, key_vecs, values, segments, log_totals, grad_mixture):

    def per_sequence(parts_in):
        return attend_back_sequence(
            parts_in[0], parts_in[1], parts_in[2], parts_in[3], parts_in[4], parts_in[5]
        )

    grad_queries, grad_keys, grad_values = lax.map(
        per_sequence,
        (
            by_sequence(queries),
            by_sequence(key_vecs),
            by_sequence(values),
            by_sequence(segments),
            log_totals,
            by_sequence(grad_mixture),
        ),
    )
    return (
        grad_queries.reshape(queries.shape),
        grad_keys.reshape(queries.shape),
        grad_values.reshape(queries.shape),
    )


def shards(
    tokens,
    segment_ids,
    norm_one,
    qkv_weight,
    attn_out_weight,
    norm_two,
    in_weight,
    out_weight,
    cotangent,
):
    feat_local = tokens.shape[1]
    heads_local = qkv_weight.shape[2]
    head_size = qkv_weight.shape[3]
    hidden_local = in_weight.shape[2]
    qkv_flat = qkv_weight.reshape(feat_local, 3 * heads_local * head_size)
    in_flat = in_weight.reshape(feat_local, 2 * hidden_local)
    residual = tokens.astype(jnp.float32)
    normed, unit_one, inverse_one = norm_forward(residual, norm_one)
    normed_gathered, joined = project_in(normed.astype(jnp.bfloat16), qkv_flat)
    seq_tokens = joined.shape[0]
    joined = joined.reshape(seq_tokens, 3, heads_local, head_size)
    cos_tab, sin_tab = rotary_tables(SEQ, head_size)
    repeats = seq_tokens // SEQ
    cos_all = jnp.tile(cos_tab, (repeats, 1))
    sin_all = jnp.tile(sin_tab, (repeats, 1))

    def turn_rows(values_in):
        return rotate(values_in, cos_all, sin_all)

    queries = turn_rows(joined[:, 0]).astype(jnp.bfloat16)
    key_vecs = turn_rows(joined[:, 1]).astype(jnp.bfloat16)
    values = joined[:, 2].astype(jnp.bfloat16)
    my_segments = lax.dynamic_slice_in_dim(
        segment_ids, lax.axis_index("col") * seq_tokens, seq_tokens, 0
    )
    mixture, log_totals = attend_all(queries, key_vecs, values, my_segments)
    mixture_flat = mixture.reshape(seq_tokens, heads_local * head_size)
    mixture_gathered, attn_part = project_out(mixture_flat, attn_out_weight)
    hidden = residual + attn_part
    normed_two, unit_two, inverse_two = norm_forward(hidden, norm_two)
    normed_two_gathered, before = project_in(normed_two.astype(jnp.bfloat16), in_flat)
    before = before.reshape(seq_tokens, 2, hidden_local)

    def gated_unit(pre_acts):
        return jax.nn.gelu(pre_acts[:, 0], approximate=False) * pre_acts[:, 1]

    active, gated_back = jax.vjp(gated_unit, before)
    active_gathered, ffn_part = project_out(active.astype(jnp.bfloat16), out_weight)
    result = (hidden + ffn_part).astype(jnp.bfloat16)
    grad_active, grad_out_weight = back_out(cotangent, active_gathered, out_weight)
    grad_before = (
        gated_back(grad_active)[0].astype(jnp.bfloat16).reshape(seq_tokens, 2 * hidden_local)
    )
    grad_normed_two, grad_in_weight = back_in(grad_before, normed_two_gathered, in_flat)
    branch_two, gain_two = norm_backward(grad_normed_two, unit_two, inverse_two, norm_two)
    grad_hidden = cotangent.astype(jnp.float32) + branch_two
    grad_mixture, grad_attn_weight = back_out(
        grad_hidden.astype(jnp.bfloat16), mixture_gathered, attn_out_weight
    )
    grad_mixture = grad_mixture.astype(jnp.bfloat16).reshape(seq_tokens, heads_local, head_size)
    grad_queries, grad_keys, grad_values = attend_back_all(
        queries, key_vecs, values, my_segments, log_totals, grad_mixture
    )
    rotate_back = jax.vjp(turn_rows, joined[:, 0])[1]
    grad_joined = jnp.stack(
        [rotate_back(grad_queries)[0], rotate_back(grad_keys)[0], grad_values], 1
    )
    grad_joined = grad_joined.astype(jnp.bfloat16).reshape(seq_tokens, 3 * heads_local * head_size)
    grad_normed, grad_qkv_weight = back_in(grad_joined, normed_gathered, qkv_flat)
    branch_one, gain_one = norm_backward(grad_normed, unit_one, inverse_one, norm_one)
    grad_tokens = grad_hidden + branch_one
    grad_qkv_weight, grad_attn_weight, grad_in_weight, grad_out_weight = lax.psum(
        (grad_qkv_weight, grad_attn_weight, grad_in_weight, grad_out_weight), "dp"
    )
    gain_one, gain_two = lax.psum((gain_one, gain_two), ("dp", "row"))
    return (
        result,
        grad_tokens,
        gain_one,
        grad_qkv_weight.reshape(qkv_weight.shape),
        grad_attn_weight,
        gain_two,
        grad_in_weight.reshape(in_weight.shape),
        grad_out_weight,
    )


def solution(mesh):
    return jax.shard_map(
        shards,
        mesh=mesh,
        in_specs=(
            P(("dp", "row"), "col"),
            P("dp"),
            P("col"),
            P("col", None, "row", None),
            P("row", "col"),
            P("col"),
            P("col", None, "row"),
            P("row", "col"),
            P(("dp", "row"), "col"),
        ),
        out_specs=(
            P(("dp", "row"), "col"),
            P(("dp", "row"), "col"),
            P("col"),
            P("col", None, "row", None),
            P("row", "col"),
            P("col"),
            P("col", None, "row"),
            P("row", "col"),
        ),
        check_vma=False,
    )
```

profile of v0, /device:TPU:0, one launch (start us, length us, event | category | flops | bytes accessed | tf_op | source)
XLA Modules:
  0.0 3376.5 jit_solution(12032146939145795582)
XLA Ops:
  9.6 9.6 all-reduce.14
  23.0 58.6 %all-gather.9.cloned.1.call-done = bf16[8192,512]{1,0:T(8,128)(2,1)} async-done(((bf16[2048,512]{1,0:T(8,128)(2,1)}), bf16[8192,512]{1,0:T(8,128)(2,1)}) %all-gather.9.cloned.1.call-update) | async-done | bytes 8388624 | tf_op jit(solution)/shard_map/all_gather | solution.py:48
  81.6 14.9 fusion.92
  102.0 274.0 %reduce-scatter.9.cloned.1.call-done = f32[4096,768]{1,0:T(8,128)} async-done(((f32[8192,768]{1,0:T(8,128)}), f32[4096,768]{1,0:T(8,128)}) %reduce-scatter.9.cloned.1.call-update) | async-done | bytes 12582928 | tf_op jit(solution)/shard_map/reduce_scatter | solution.py:49
  376.1 12.6 copy.22
  411.5 111.5 %while.50 = (s32[]{:T(128)}, bf16[8,512,4,64]{1,3,2,0:T(8,128)(2,1)}, f32[8,4,512]{2,1,0:T(4,128)}, s32[8]{0:T(128)S(1)}, bf16[4224,4,64]{0,2,1:T(8,128)(2,1)}, ...) while((s32[]{:T(128)}, ...), condition=%wide.region_8.9_spmd, body=%wide.region_5.8_spmd.sunk | while | flops 353368064 | bytes 18299660 | solution.py:150
  528.2 56.7 %all-gather.11.cloned.1.call-done = bf16[8192,256]{0,1:T(8,128)(2,1)} async-done(((bf16[4096,256]{0,1:T(8,128)(2,1)}), bf16[8192,256]{0,1:T(8,128)(2,1)}) %all-gather.11.cloned.1.call-update) | async-done | bytes 4194320 | tf_op jit(solution)/shard_map/all_gather | solution.py:59
  584.9 10.3 fusion.93
  595.9 125.6 %reduce-scatter.11.cloned.1.call-done = f32[2048,512]{1,0:T(8,128)} async-done(((f32[8192,512]{1,0:T(8,128)}), f32[2048,512]{1,0:T(8,128)}) %reduce-scatter.11.cloned.1.call-update) | async-done | bytes 4194320 | tf_op jit(solution)/shard_map/reduce_scatter | solution.py:60
  726.2 8.1 all-reduce.13
  738.3 43.1 %all-gather.17.cloned.1.call-done = bf16[8192,512]{1,0:T(8,128)(2,1)} async-done(((bf16[2048,512]{1,0:T(8,128)(2,1)}), bf16[8192,512]{1,0:T(8,128)(2,1)}) %all-gather.17.cloned.1.call-update) | async-done | bytes 8388624 | tf_op jit(solution)/shard_map/all_gather | solution.py:70
  781.4 16.0 fusion.96
  797.4 44.4 %all-gather.13.cloned.1.call-done = bf16[8192,512]{1,0:T(8,128)(2,1)} async-done(((bf16[2048,512]{1,0:T(8,128)(2,1)}), bf16[8192,512]{1,0:T(8,128)(2,1)}) %all-gather.13.cloned.1.call-update) | async-done | bytes 8388624 | tf_op jit(solution)/shard_map/all_gather | solution.py:48
  841.8 22.3 fusion.94
  864.4 219.7 %reduce-scatter.17.cloned.1.call-done = f32[4096,656]{0,1:T(8,128)} async-done(((f32[8192,656]{0,1:T(8,128)}), f32[4096,656]{0,1:T(8,128)}) %reduce-scatter.17.cloned.1.call-update) | async-done | bytes 10747920 | tf_op jit(solution)/shard_map/reduce_scatter | solution.py:72
  1084.1 472.6 %reduce-scatter.13.cloned.1.call-done = f32[4096,1312]{0,1:T(8,128)} async-done(((f32[8192,1312]{0,1:T(8,128)}), f32[4096,1312]{0,1:T(8,128)}) %reduce-scatter.13.cloned.1.call-update) | async-done | bytes 21495824 | tf_op jit(solution)/shard_map/reduce_scatter | solution.py:49
  1556.7 26.5 multiply_bitcast_fusion
  1583.2 14.9 fusion.52
  1598.1 11.8 add_convert_fusion
  1610.6 252.7 %all-gather.19.cloned.1.call-done = bf16[8192,1312]{0,1:T(8,128)(2,1)} async-done(((bf16[4096,1312]{0,1:T(8,128)(2,1)}), bf16[8192,1312]{0,1:T(8,128)(2,1)}) %all-gather.19.cloned.1.call-update) | async-done | bytes 21495824 | tf_op jit(solution)/shard_map/all_gather | solution.py:79
  1863.3 21.3 fusion.97
  1885.0 112.1 %all-gather.15.cloned.1.call-done = bf16[8192,656]{0,1:T(8,128)(2,1)} async-done(((bf16[4096,656]{0,1:T(8,128)(2,1)}), bf16[8192,656]{0,1:T(8,128)(2,1)}) %all-gather.15.cloned.1.call-update) | async-done | bytes 10747920 | tf_op jit(solution)/shard_map/all_gather | solution.py:59
  1997.2 16.6 fusion.95
  2013.9 112.3 %reduce-scatter.19.cloned.1.call-done = f32[2048,512]{1,0:T(8,128)} async-done(((f32[8192,512]{1,0:T(8,128)}), f32[2048,512]{1,0:T(8,128)}) %reduce-scatter.19.cloned.1.call-update) | async-done | bytes 4194320 | tf_op jit(solution)/shard_map/reduce_scatter | solution.py:81
  2131.1 8.0 all-reduce.12
  2139.1 115.6 %reduce-scatter.15.cloned.1.call-done = f32[2048,512]{1,0:T(8,128)} async-done(((f32[8192,512]{1,0:T(8,128)}), f32[2048,512]{1,0:T(8,128)}) %reduce-scatter.15.cloned.1.call-update) | async-done | bytes 4194320 | tf_op jit(solution)/shard_map/reduce_scatter | solution.py:60
  2254.7 7.5 fusion.88
  2262.3 58.4 %all-gather.21.cloned.1.call-done = bf16[8192,512]{1,0:T(8,128)(2,1)} async-done(((bf16[2048,512]{1,0:T(8,128)(2,1)}), bf16[8192,512]{1,0:T(8,128)(2,1)}) %all-gather.21.cloned.1.call-update) | async-done | bytes 8388624 | tf_op jit(solution)/shard_map/all_gather | solution.py:70
  2320.7 9.1 fusion.98
  2330.1 99.2 %reduce-scatter.21.cloned.1.call-done = f32[4096,256]{1,0:T(8,128)} async-done(((f32[8192,256]{1,0:T(8,128)}), f32[4096,256]{1,0:T(8,128)}) %reduce-scatter.21.cloned.1.call-update) | async-done | bytes 4194320 | tf_op jit(solution)/shard_map/reduce_scatter | solution.py:72
  2439.2 386.5 %while.51 = (s32[]{:T(128)}, f32[4224,4,64]{0,2,1:T(8,128)}, f32[4224,4,64]{0,2,1:T(8,128)}, f32[8,512,4,64]{1,0,3,2:T(8,128)}, s32[8]{0:T(128)S(1)}, /*index=5*...) while((s32[]{:T(128)}, f32[4224,4,64]{0,2,1:T(8,128)}, ...), condition=%wide.region_25.26_spmd, body=%wide.region_23.25_spmd.sunk | while | flops 861108224 | bytes 76814224 | solution.py:202
  2462.0 11.5 dynamic_update_slice.57
  2510.5 11.5 dynamic_update_slice.57
  2559.1 11.5 dynamic_update_slice.57
  2607.6 11.5 dynamic_update_slice.57
  2656.2 11.5 dynamic_update_slice.57
  2704.7 11.5 dynamic_update_slice.57
  2753.2 11.5 dynamic_update_slice.57
  2801.5 11.5 dynamic_update_slice.57
  2846.2 152.6 %all-gather.23.cloned.1.call-done = bf16[8192,768]{0,1:T(8,128)(2,1)} async-done(((bf16[4096,768]{0,1:T(8,128)(2,1)}), bf16[8192,768]{0,1:T(8,128)(2,1)}) %all-gather.23.cloned.1.call-update) | async-done | bytes 12582928 | tf_op jit(solution)/shard_map/all_gather | solution.py:79
  2998.8 15.0 fusion.99
  3014.0 12.1 fusion.101
  3026.1 23.4 fusion.103
  3052.6 13.2 fusion.102
  3065.8 74.4 %reduce-scatter.23.cloned.1.call-done = f32[2048,512]{1,0:T(8,128)} async-done(((f32[8192,512]{1,0:T(8,128)}), f32[2048,512]{1,0:T(8,128)}) %reduce-scatter.23.cloned.1.call-update) | async-done | bytes 4194320 | tf_op jit(solution)/shard_map/reduce_scatter | solution.py:81
  3143.8 34.0 %all-reduce.9 = (f32[512]{0:T(512)}, f32[512]{0:T(512)}) all-reduce(f32[512]{0:T(512)S(1)} %get-tuple-element.320, f32[512]{0:T(512)S(1)} %copy-done.25), channel_id=1, replica_groups=mesh['dp'=4,'row'=4,'col'=2] {'dp','row'}, use_global_device_ids=true, to_apply=%region_32.33 | all-reduce | flops 1024 | bytes 8192 | tf_op jit(solution)/shard_map/psum | solution.py:328
  3177.9 8.0 all-reduce.11
  3191.4 170.9 %all-reduce.17.cloned.1.call-done = (f32[512,3,4,64]{0,3,2,1:T(8,128)}, f32[256,512]{1,0:T(8,128)}, f32[512,2,656]{0,2,1:T(8,128)}, f32[656,512]{1,0:T(8,128)}) async-done(((f32[512,3,4,64]{0,3,2,1:T(8,128)}, f32[256,512]{1,0:T(8,128)}, f32[512,2,656]{0,2,1:T(8,128)}, f32[656,512]{1,0:T(8,128)}), (f32[512,3,4,64]{0,3,2,1:T(8,128)}, f32[256,512]{1,0:T(8,128)}, f32[512,2,656]{0,2,1:T(8,128)}, ...) | async-done | bytes 6127632 | tf_op jit(solution)/shard_map/psum | solution.py:325
  (382 shorter events, 438.4 us)
Async XLA Ops:
  7.2 834.6 %copy-start = (bf16[512,2,656]{0,2,1:T(8,128)(2,1)S(1)}, bf16[512,2,656]{0,2,1:T(8,128)(2,1)}, u32[]{:S(2)}) copy-start(bf16[512,2,656]{0,2,1:T(8,128)(2,1)} %param.19) | copy-start | bytes 4030468
  7.2 74.4 %copy-start.26 = (bf16[512,3,4,64]{0,3,2,1:T(8,128)(2,1)S(1)}, bf16[512,3,4,64]{0,3,2,1:T(8,128)(2,1)}, u32[]{:S(2)}) copy-start(bf16[512,3,4,64]{0,3,2,1:T(8,128)(2,1)} %param.16) | copy-start | bytes 2359300
  7.2 74.4 %all-gather.9.cloned.1.call-start = ((), (), s32[]{:S(2)}) async-start(), calls=%async_computation.8 | async-start | bytes 10485760 | tf_op jit(solution)/shard_map/all_gather | solution.py:48
  22.9 353.1 %reduce-scatter.9.cloned.1.call-start = ((), (), s32[]{:S(2)}) async-start(), calls=%async_computation.9 | async-start | bytes 37748736 | tf_op jit(solution)/shard_map/reduce_scatter | solution.py:49
  96.6 488.3 %all-gather.11.cloned.1.call-start = ((), (), s32[]{:S(2)}) async-start(), calls=%async_computation.10 | async-start | bytes 6291456 | tf_op jit(solution)/shard_map/all_gather | solution.py:59
  388.7 7.0 copy-start.3
  523.0 5.0 copy-start.17
  523.0 5.0 copy-start.29
  525.8 59.1 %copy-start.15 = (bf16[256,512]{1,0:T(8,128)(2,1)S(1)}, bf16[256,512]{1,0:T(8,128)(2,1)}, u32[]{:S(2)}) copy-start(bf16[256,512]{1,0:T(8,128)(2,1)} %param.17) | copy-start | bytes 786436
  528.0 193.5 %reduce-scatter.11.cloned.1.call-start = ((), (), s32[]{:S(2)}) async-start(), calls=%async_computation.11 | async-start | bytes 20971520 | tf_op jit(solution)/shard_map/reduce_scatter | solution.py:60
  595.2 126.3 %copy-start.4 = (bf16[2048,512]{1,0:T(8,128)(2,1)S(1)}, bf16[2048,512]{1,0:T(8,128)(2,1)}, u32[]{:S(2)}) copy-start(bf16[2048,512]{1,0:T(8,128)(2,1)} %param.13) | copy-start | bytes 6291460
  595.3 186.1 %all-gather.17.cloned.1.call-start = ((), (), s32[]{:S(2)}) async-start(), calls=%async_computation.16 | async-start | bytes 10485760 | tf_op jit(solution)/shard_map/all_gather | solution.py:70
  595.9 138.4 %copy-start.22 = (f32[512]{0:T(512)S(1)}, f32[512]{0:T(512)}, u32[]{:S(2)}) copy-start(f32[512]{0:T(512)} %param.18) | copy-start | bytes 6148
  595.9 245.9 %all-gather.13.cloned.1.call-start = ((), (), s32[]{:S(2)}) async-start(), calls=%async_computation.12 | async-start | bytes 10485760 | tf_op jit(solution)/shard_map/all_gather | solution.py:48
  734.3 47.1 %copy-start.28 = (bf16[656,512]{1,0:T(8,128)(2,1)S(1)}, bf16[656,512]{1,0:T(8,128)(2,1)}, u32[]{:S(2)}) copy-start(bf16[656,512]{1,0:T(8,128)(2,1)} %param.20) | copy-start | bytes 2015236
  738.2 345.8 %reduce-scatter.17.cloned.1.call-start = ((), (), s32[]{:S(2)}) async-start(), calls=%async_computation.17 | async-start | bytes 32243712 | tf_op jit(solution)/shard_map/reduce_scatter | solution.py:72
  797.4 759.3 %reduce-scatter.13.cloned.1.call-start = ((), (), s32[]{:S(2)}) async-start(), calls=%async_computation.13 | async-start | bytes 64487424 | tf_op jit(solution)/shard_map/reduce_scatter | solution.py:49
  864.1 999.2 %all-gather.19.cloned.1.call-start = ((), (), s32[]{:S(2)}) async-start(), calls=%async_computation.18 | async-start | bytes 32243712 | tf_op jit(solution)/shard_map/all_gather | solution.py:79
  1556.7 26.5 copy-start.6
  1610.0 387.2 %all-gather.15.cloned.1.call-start = ((), (), s32[]{:S(2)}) async-start(), calls=%async_computation.14 | async-start | bytes 16121856 | tf_op jit(solution)/shard_map/all_gather | solution.py:59
  1610.6 515.6 %reduce-scatter.19.cloned.1.call-start = ((), (), s32[]{:S(2)}) async-start(), calls=%async_computation.19 | async-start | bytes 20971520 | tf_op jit(solution)/shard_map/reduce_scatter | solution.py:81
  1884.6 370.2 %reduce-scatter.15.cloned.1.call-start = ((), (), s32[]{:S(2)}) async-start(), calls=%async_computation.15 | async-start | bytes 20971520 | tf_op jit(solution)/shard_map/reduce_scatter | solution.py:60
  2013.8 240.9 %copy-start.10 = (bf16[2048,512]{1,0:T(8,128)(2,1)S(1)}, bf16[2048,512]{1,0:T(8,128)(2,1)}, u32[]{:S(2)}) copy-start(bf16[2048,512]{1,0:T(8,128)(2,1)} %param.21) | copy-start | bytes 6291460
  2013.8 306.9 %all-gather.21.cloned.1.call-start = ((), (), s32[]{:S(2)}) async-start(), calls=%async_computation.20 | async-start | bytes 10485760 | tf_op jit(solution)/shard_map/all_gather | solution.py:70
  2139.1 181.6 %copy-start.16 = (bf16[256,512]{1,0:T(8,128)(2,1)S(1)}, bf16[256,512]{1,0:T(8,128)(2,1)}, u32[]{:S(2)}) copy-start(bf16[256,512]{1,0:T(8,128)(2,1)} %param.17) | copy-start | bytes 786436
  2262.2 167.0 %reduce-scatter.21.cloned.1.call-start = ((), (), s32[]{:S(2)}) async-start(), calls=%async_computation.21 | async-start | bytes 12582912 | tf_op jit(solution)/shard_map/reduce_scatter | solution.py:72
  2329.8 669.0 %all-gather.23.cloned.1.call-start = ((), (), s32[]{:S(2)}) async-start(), calls=%async_computation.22 | async-start | bytes 18874368 | tf_op jit(solution)/shard_map/all_gather | solution.py:79
  2450.3 6.2 slice-start
  2498.8 6.2 slice-start
  2547.4 6.2 slice-start
  2596.0 6.2 slice-start
  2644.5 6.2 slice-start
  2693.0 6.2 slice-start
  2741.5 6.2 slice-start
  2789.8 6.1 slice-start
  2825.7 5.3 copy-start.8
  2846.1 152.7 %copy-start.27 = (bf16[512,3,4,64]{0,3,2,1:T(8,128)(2,1)S(1)}, bf16[512,3,4,64]{0,3,2,1:T(8,128)(2,1)}, u32[]{:S(2)}) copy-start(bf16[512,3,4,64]{0,3,2,1:T(8,128)(2,1)} %param.16) | copy-start | bytes 2359300
  2846.2 294.1 %reduce-scatter.23.cloned.1.call-start = ((), (), s32[]{:S(2)}) async-start(), calls=%async_computation.23 | async-start | bytes 20971520 | tf_op jit(solution)/shard_map/reduce_scatter | solution.py:81
  3013.9 348.4 %all-reduce.17.cloned.1.call-start = ((), (), s32[]{:S(2)}) async-start(), calls=%async_computation.24 | async-start | bytes 12255232 | tf_op jit(solution)/shard_map/psum | solution.py:325
  3013.9 35.5 %slice-start.4 = ((s8[8388608]{0:T(1024)(128)(4,1)}), s8[4194304]{0:T(1024)(128)(4,1)S(1)}, s32[]{:S(2)}) async-start(s8[8388608]{0:T(1024)(128)(4,1)} %bitcast.202), calls=%async_computation.29 | async-start | bytes 8388608
  3026.1 23.4 slice-start.5
  3026.1 23.4 copy-start.12
  3065.7 74.5 %copy-start.5 = (bf16[2048,512]{1,0:T(8,128)(2,1)S(1)}, bf16[2048,512]{1,0:T(8,128)(2,1)}, u32[]{:S(2)}) copy-start(bf16[2048,512]{1,0:T(8,128)(2,1)} %param.13) | copy-start | bytes 6291460
  3065.7 74.5 %copy-start.19 = (f32[2048]{0:T(1024)S(1)}, f32[2048]{0:T(1024)}, u32[]{:S(2)}) copy-start(f32[2048]{0:T(1024)} %copy-done.18) | copy-start | bytes 24580
  3065.7 74.5 %copy-start.21 = (f32[2048]{0:T(1024)S(1)}, f32[2048]{0:T(1024)}, u32[]{:S(2)}) copy-start(f32[2048]{0:T(1024)} %copy-done.20) | copy-start | bytes 24580
  3065.7 74.5 %copy-start.23 = (f32[512]{0:T(512)S(1)}, f32[512]{0:T(512)}, u32[]{:S(2)}) copy-start(f32[512]{0:T(512)} %param.15) | copy-start | bytes 6148
  3065.8 78.0 %copy-start.25 = (f32[512]{0:T(512)S(1)}, f32[512]{0:T(512)}, u32[]{:S(2)}) copy-start(f32[512]{0:T(512)} %get-tuple-element.318) | copy-start | bytes 6148
  3362.3 6.3 copy-start.14
  (27 other events, 86.1 us)
Sparse Core Ops, SparseCore 0:
  23.1 58.5 all-gather.8
  96.7 279.3 reduce-scatter.8
  528.1 56.7 all-gather.10
  595.4 126.1 reduce-scatter.10
  723.0 58.2 all-gather.16
  783.4 58.2 all-gather.12
  844.2 239.8 reduce-scatter.16
  1086.5 470.1 reduce-scatter.12
  1610.1 253.1 all-gather.18
  1864.8 132.3 all-gather.14
  1999.9 126.1 reduce-scatter.18
  2128.6 126.1 reduce-scatter.14
  2262.4 58.2 all-gather.20
  2330.0 99.2 reduce-scatter.20
  2846.3 152.5 all-gather.22
  3014.0 126.1 reduce-scatter.22
  3143.4 218.8 all-reduce.16
where the time goes:
time: 3390 us; the launch traced here: 3380 us
  waiting for transfers between devices  2440 us (72%)
  matrix products  374 us (11%)
  local copies, waits for them, and re-layouts  251 us (7%)
  other arithmetic  150 us (4%)
  loops' own time  73.2 us (2%)
  blocking collectives  67.8 us (2%)
    reduce_scatter x2, waiting for transfers between devices, project_in(): lax.psum_scatter(jnp.dot(gathered, weight_flat, preferred_element_type=jn...  747 us
    all_gather x2, waiting for transfers between devices, back_in(): gathered = lax.all_gather(grad_low, 'col', axis=0, tiled=True)  405 us
    reduce_scatter x2, waiting for transfers between devices, back_out(): lax.psum_scatter(contract_cols(gathered, weight), 'col', scatter_dimensio...  319 us
    reduce_scatter x2, waiting for transfers between devices, project_out(): lax.psum_scatter(jnp.dot(gathered, weight, preferred_element_type=jnp.flo...  241 us
    reduce_scatter x2, waiting for transfers between devices, back_in(): lax.psum_scatter(contract_cols(gathered, weight_flat), 'row', scatter_dim...  187 us
    psum x1, waiting for transfers between devices, shards(): lax.psum((grad_qkv_weight, grad_attn_weight, grad_in_weight, grad_out_wei...  171 us
    all_gather x2, waiting for transfers between devices, project_out(): gathered = lax.all_gather(acts_low, 'col', axis=0, tiled=True)  169 us
    all_gather x2, waiting for transfers between devices, project_in(): gathered = lax.all_gather(normed_low, 'row', axis=0, tiled=True)  103 us
  transfers between devices with their start and end apart: 17, of which 17 were waited for; matrix products, arithmetic and copies ran while one was open for 5% of the time, Pallas kernels for 0%

commit v1 on v0

v1 whole, which is shorter than its diff:
```python
import functools

import jax
import jax.numpy as jnp
from jax import lax
from jax.experimental import pallas as pl
from jax.experimental.pallas import tpu as pltpu
from jax.sharding import PartitionSpec as P

WINDOW = 128
HALF = WINDOW // 2
SEQ = 4096
BLOCK = 128
PAIR = 128

EPS = 1e-05
NEG = -1e30
THETA = 10000.0
PLANE = ("row", "col")
VMEM_LIMIT = 48 * 1024 * 1024


def dot_nn(left, right):
    return jnp.dot(left, right, preferred_element_type=jnp.float32)


def dot_nt(left, right):
    return lax.dot_general(
        left, right, (((1,), (1,)), ((), ())), preferred_element_type=jnp.float32
    )


def dot_tn(left, right):
    return lax.dot_general(
        left, right, (((0,), (0,)), ((), ())), preferred_element_type=jnp.float32
    )


def first_half(shape):
    return lax.broadcasted_iota(jnp.int32, shape, 1) % 64 < 32


def turn(values_in):
    ahead = pltpu.roll(values_in, PAIR - 32, 1)
    behind = pltpu.roll(values_in, 32, 1)
    return jnp.where(first_half(values_in.shape), -ahead, behind)


def turn_back(values_in):
    ahead = pltpu.roll(values_in, PAIR - 32, 1)
    behind = pltpu.roll(values_in, 32, 1)
    return jnp.where(first_half(values_in.shape), ahead, -behind)


def forward_kernel(
    blocks, normed_ref, wq_ref, wk_ref, wv_ref, cos_ref, sin_ref, bias_ref, q_ref, k_ref, v_ref, mix_ref
):
    cos_tab = cos_ref[...]
    sin_tab = sin_ref[...]
    own = pl.ds(HALF, blocks * BLOCK)
    queries = dot_nn(normed_ref[own, :], wq_ref[...])
    queries = queries * cos_tab[HALF:-HALF] + turn(queries) * sin_tab[HALF:-HALF]
    q_ref[...] = queries.astype(jnp.bfloat16) * jnp.bfloat16(0.125)
    keys = dot_nn(normed_ref[...], wk_ref[...])
    keys = keys * cos_tab + turn(keys) * sin_tab
    k_ref[...] = keys.astype(jnp.bfloat16)
    v_ref[...] = dot_nn(normed_ref[...], wv_ref[...]).astype(jnp.bfloat16)
    lower = lax.broadcasted_iota(jnp.int32, (BLOCK, PAIR), 1) < 64
    for block in range(blocks):
        rows = pl.ds(block * BLOCK, BLOCK)
        span = pl.ds(block * BLOCK, BLOCK + WINDOW)
        q_blk = q_ref[rows, :]
        k_blk = k_ref[span, :]
        v_blk = v_ref[span, :]
        bias = bias_ref[rows, :]
        outs = []
        for head in range(2):
            q_head = jnp.where(lower if head == 0 else ~lower, q_blk, jnp.bfloat16(0))
            scores = dot_nt(q_head, k_blk) + bias
            weights = jnp.exp(scores - jnp.max(scores, -1, keepdims=True))
            probs = weights * (1.0 / jnp.sum(weights, -1, keepdims=True))
            outs.append(dot_nn(probs.astype(jnp.bfloat16), v_blk))
        mix_ref[rows, :] = jnp.where(lower, outs[0], outs[1]).astype(jnp.bfloat16)


def backward_kernel(
    blocks, q_ref, k_ref, v_ref, grad_ref, cos_ref, sin_ref, bias_ref, dq_ref, dk_ref, dv_ref, dk_acc, dv_acc
):
    dk_acc[...] = jnp.zeros_like(dk_acc)
    dv_acc[...] = jnp.zeros_like(dv_acc)
    lower = lax.broadcasted_iota(jnp.int32, (BLOCK, PAIR), 1) < 64
    for block in range(blocks):
        rows = pl.ds(block * BLOCK, BLOCK)
        span = pl.ds(block * BLOCK, BLOCK + WINDOW)
        own = pl.ds(block * BLOCK + HALF, BLOCK)
        q_blk = q_ref[rows, :]
        k_blk = k_ref[span, :]
        v_blk = v_ref[span, :]
        g_blk = grad_ref[rows, :]
        bias = bias_ref[rows, :]
        dq_parts = []
        dk_part = 0.0
        dv_part = 0.0
        for head in range(2):
            mask = lower if head == 0 else ~lower
            q_head = jnp.where(mask, q_blk, jnp.bfloat16(0))
            g_head = jnp.where(mask, g_blk, jnp.bfloat16(0))
            scores = dot_nt(q_head, k_blk) + bias
            weights = jnp.exp(scores - jnp.max(scores, -1, keepdims=True))
            probs = weights * (1.0 / jnp.sum(weights, -1, keepdims=True))
            grad_probs = dot_nt(g_head, v_blk)
            centre = jnp.sum(grad_probs * probs, -1, keepdims=True)
            grad_scores = (probs * (grad_probs - centre)).astype(jnp.bfloat16)
            dq_parts.append(dot_nn(grad_scores, k_blk))
            dk_part += dot_tn(grad_scores, q_head)
            dv_part += dot_tn(probs.astype(jnp.bfloat16), g_head)
        dk_acc[span, :] += dk_part
        dv_acc[span, :] += dv_part
        dq = jnp.where(lower, dq_parts[0], dq_parts[1]) * 0.125
        dq = dq * cos_ref[own, :] + turn_back(dq * sin_ref[own, :])
        dq_ref[rows, :] = dq.astype(jnp.bfloat16)
    dk = dk_acc[...]
    dk_ref[...] = (dk * cos_ref[...] + turn_back(dk * sin_ref[...])).astype(jnp.bfloat16)
    dv_ref[...] = dv_acc[...].astype(jnp.bfloat16)


def column_block(rows, first=0):
    return pl.BlockSpec((rows, PAIR), lambda pair: (0, first + pair))


def whole_block(shape):
    return pl.BlockSpec(shape, lambda pair: (0,) * len(shape))


def attend(normed_ext, qkv_full, cos_tab, sin_tab, bias):
    ext, width = normed_ext.shape
    count = ext - 2 * HALF
    pairs = width // PAIR
    kind = jnp.bfloat16
    return pl.pallas_call(
        functools.partial(forward_kernel, count // BLOCK),
        grid=(pairs,),
        in_specs=[
            whole_block(normed_ext.shape),
            column_block(width),
            column_block(width, pairs),
            column_block(width, 2 * pairs),
            whole_block(cos_tab.shape),
            whole_block(sin_tab.shape),
            whole_block(bias.shape),
        ],
        out_specs=[column_block(count), column_block(ext), column_block(ext), column_block(count)],
        out_shape=[
            jax.ShapeDtypeStruct((count, width), kind),
            jax.ShapeDtypeStruct((ext, width), kind),
            jax.ShapeDtypeStruct((ext, width), kind),
            jax.ShapeDtypeStruct((count, width), kind),
        ],
        compiler_params=pltpu.CompilerParams(vmem_limit_bytes=VMEM_LIMIT),
        cost_estimate=pl.CostEstimate(
            flops=2 * ext * width * 3 * width + 4 * count * 256 * 128 * 16,
            bytes_accessed=2 * (3 * width * width + 5 * ext * width),
            transcendentals=count * 256 * 16,
        ),
        name="attend_forward",
    )(normed_ext, qkv_full, qkv_full, qkv_full, cos_tab, sin_tab, bias)


def attend_back(queries, keys, values, grad_mixture, cos_tab, sin_tab, bias):
    ext, width = keys.shape
    count = ext - 2 * HALF
    kind = jnp.bfloat16
    return pl.pallas_call(
        functools.partial(backward_kernel, count // BLOCK),
        grid=(width // PAIR,),
        in_specs=[
            column_block(count),
            column_block(ext),
            column_block(ext),
            column_block(count),
            whole_block(cos_tab.shape),
            whole_block(sin_tab.shape),
            whole_block(bias.shape),
        ],
        out_specs=[column_block(count), column_block(ext), column_block(ext)],
        out_shape=[
            jax.ShapeDtypeStruct((count, width), kind),
            jax.ShapeDtypeStruct((ext, width), kind),
            jax.ShapeDtypeStruct((ext, width), kind),
        ],
        scratch_shapes=[pltpu.VMEM((ext, PAIR), jnp.float32), pltpu.VMEM((ext, PAIR), jnp.float32)],
        compiler_params=pltpu.CompilerParams(vmem_limit_bytes=VMEM_LIMIT),
        cost_estimate=pl.CostEstimate(
            flops=12 * count * 256 * 128 * 16,
            bytes_accessed=2 * 7 * ext * width,
            transcendentals=count * 256 * 16,
        ),
        name="attend_backward",
    )(queries, keys, values, grad_mixture, cos_tab, sin_tab, bias)


def unit_rows(inputs):
    average = jnp.mean(inputs, 1, keepdims=True)
    centred = inputs - average
    inverse_std = lax.rsqrt(jnp.mean(centred * centred, 1, keepdims=True) + EPS)
    return centred * inverse_std, inverse_std


def norm_backward(grad_normed, unit, inverse_std, gain_vec):
    scaled = grad_normed * gain_vec
    average = jnp.mean(scaled, 1, keepdims=True)
    cross = jnp.mean(scaled * unit, 1, keepdims=True)
    return inverse_std * (scaled - average - unit * cross), jnp.sum(grad_normed * unit, 0)


def whole_rows(array_in):
    return lax.all_to_all(array_in, "col", 0, 1, tiled=True)


def split_rows(array_in):
    return lax.all_to_all(array_in, "col", 1, 0, tiled=True)


def gather_plane(local):
    return lax.all_gather(local, PLANE, axis=0, tiled=False)


def sum_plane(stacked):
    part = lax.psum_scatter(stacked, PLANE, scatter_dimension=0, tiled=False)
    return lax.psum(part, "dp").astype(jnp.float32)


def gelu_parts(pre):
    cdf = 0.5 * (1.0 + lax.erf(pre * 0.7071067811865476))
    slope = cdf + pre * jnp.exp(-0.5 * pre * pre) * 0.3989422804014327
    return pre * cdf, slope


def shards(
    tokens,
    segment_ids,
    norm_one,
    qkv_weight,
    attn_out_weight,
    norm_two,
    in_weight,
    out_weight,
    cotangent,
):
    rows, cols = lax.axis_size("row"), lax.axis_size("col")
    plane = rows * cols
    place = lax.axis_index("row") * cols + lax.axis_index("col")
    feat = tokens.shape[1]
    width = feat * cols
    heads_width = qkv_weight.shape[2] * qkv_weight.shape[3]
    hidden = in_weight.shape[2]
    low = jnp.bfloat16

    qkv_stack = gather_plane(qkv_weight.reshape(feat, 3, heads_width))
    qkv_full = qkv_stack.reshape(rows, cols, feat, 3, heads_width)
    qkv_full = qkv_full.transpose(1, 2, 3, 0, 4).reshape(width, 3 * width)

    def out_full(local):
        stack = gather_plane(local)
        stack = stack.reshape((rows, cols) + local.shape).transpose(0, 2, 1, 3)
        return stack.reshape(rows * local.shape[0], width)

    attn_full = out_full(attn_out_weight)
    in_stack = gather_plane(in_weight.transpose(1, 2, 0))
    in_full = in_stack.reshape(rows, cols, 2, hidden, feat).transpose(2, 0, 3, 1, 4)
    in_full = in_full.reshape(2, rows * hidden, width)
    ffn_out_full = out_full(out_weight)
    gain_one, gain_two = lax.all_gather(jnp.stack([norm_one, norm_two]), "col", axis=1, tiled=True)

    own_tokens = whole_rows(tokens)
    own_cotangent = whole_rows(cotangent)
    count = own_tokens.shape[0]
    ahead = [(i, i + 1) for i in range(plane - 1)]
    behind = [(i + 1, i) for i in range(plane - 1)]
    before_rows = lax.ppermute(own_tokens[-HALF:], PLANE, ahead)
    after_rows = lax.ppermute(own_tokens[:HALF], PLANE, behind)
    residual_ext = jnp.concatenate([before_rows, own_tokens, after_rows], 0).astype(jnp.float32)
    unit_ext, inverse_ext = unit_rows(residual_ext)
    normed_ext = (unit_ext * gain_one).astype(low)
    normed_one = normed_ext[HALF:-HALF]

    total = segment_ids.shape[0]
    marks = segment_ids + 16 * (lax.iota(jnp.int32, total) // SEQ)
    marks = jnp.pad(marks, (HALF, HALF), constant_values=-1)
    marks = lax.dynamic_slice_in_dim(marks, place * count, count + 2 * HALF, 0)
    blocks = count // BLOCK
    key_marks = jnp.stack([marks[i * BLOCK : i * BLOCK + BLOCK + WINDOW] for i in range(blocks)])
    query_marks = marks[HALF:-HALF].reshape(blocks, BLOCK)
    shape = (BLOCK, BLOCK + WINDOW)
    distance = lax.broadcasted_iota(jnp.int32, shape, 1) - lax.broadcasted_iota(jnp.int32, shape, 0)
    near = jnp.abs(distance - HALF) <= HALF
    allowed = (query_marks[:, :, None] == key_marks[:, None, :]) & near[None]
    bias = jnp.where(allowed, 0.0, NEG).astype(jnp.float32).reshape(count, BLOCK + WINDOW)

    places = (place * count - HALF + lax.iota(jnp.int32, count + 2 * HALF)) % SEQ
    frequencies = THETA ** (-jnp.arange(32, dtype=jnp.float32) * 2.0 / 64)
    angles = places.astype(jnp.float32)[:, None] * frequencies[None, :]
    cos_tab = jnp.tile(jnp.cos(angles), (1, PAIR // 32))
    sin_tab = jnp.tile(jnp.sin(angles), (1, PAIR // 32))

    queries, keys, values, mixture = attend(normed_ext, qkv_full, cos_tab, sin_tab, bias)
    hidden_rows = own_tokens.astype(jnp.float32) + dot_nn(mixture, attn_full)
    unit_two, inverse_two = unit_rows(hidden_rows)
    normed_two = (unit_two * gain_two).astype(low)
    input_half = dot_nt(normed_two, in_full[0])
    gate_half = dot_nt(normed_two, in_full[1])
    grad_active = dot_nt(own_cotangent, ffn_out_full)
    gelu, slope = gelu_parts(input_half)
    active = (gelu * gate_half).astype(low)
    grad_input = (grad_active * gate_half * slope).astype(low)
    grad_gate = (grad_active * gelu).astype(low)
    active, grad_input, grad_gate = lax.optimization_barrier((active, grad_input, grad_gate))
    result = (hidden_rows + dot_nn(active, ffn_out_full)).astype(low)

    def out_stack(grad):
        grad = grad.reshape(rows, -1, cols, feat).transpose(0, 2, 1, 3)
        return grad.reshape(plane, -1, feat)

    grad_out = sum_plane(out_stack(dot_tn(active, own_cotangent).astype(low)))
    grad_in = jnp.stack([dot_tn(grad_input, normed_two), dot_tn(grad_gate, normed_two)]).astype(low)
    grad_in = grad_in.reshape(2, rows, hidden, cols, feat).transpose(1, 3, 0, 2, 4)
    grad_in = sum_plane(grad_in.reshape(plane, 2, hidden, feat)).transpose(2, 0, 1)
    grad_normed_two = dot_nn(grad_input, in_full[0]) + dot_nn(grad_gate, in_full[1])
    branch_two, sum_two = norm_backward(grad_normed_two, unit_two, inverse_two, gain_two)
    grad_hidden = own_cotangent.astype(jnp.float32) + branch_two
    grad_branch = grad_hidden.astype(low)

    grad_mixture = dot_nt(grad_branch, attn_full).astype(low)
    grad_attn = sum_plane(out_stack(dot_tn(mixture, grad_branch).astype(low)))
    dq, dk_ext, dv_ext = attend_back(queries, keys, values, grad_mixture, cos_tab, sin_tab, bias)
    edges = jnp.concatenate([dk_ext, dv_ext], 1)
    to_next = lax.ppermute(edges[-HALF:], PLANE, ahead)
    to_prev = lax.ppermute(edges[:HALF], PLANE, behind)
    middle = edges[HALF:-HALF]
    middle = jnp.concatenate(
        [
            (middle[:HALF].astype(jnp.float32) + to_next.astype(jnp.float32)).astype(low),
            middle[HALF:-HALF],
            (middle[-HALF:].astype(jnp.float32) + to_prev.astype(jnp.float32)).astype(low),
        ],
        0,
    )
    grad_joined = jnp.concatenate([dq, middle], 1)
    grad_qkv = dot_tn(normed_one, grad_joined).astype(low)
    grad_qkv = grad_qkv.reshape(cols, feat, 3, rows, heads_width).transpose(3, 0, 1, 2, 4)
    grad_qkv = sum_plane(grad_qkv.reshape(plane, feat, 3 * heads_width))
    grad_normed_one = dot_nt(grad_joined, qkv_full)
    branch_one, sum_one = norm_backward(
        grad_normed_one, unit_ext[HALF:-HALF], inverse_ext[HALF:-HALF], gain_one
    )
    grad_tokens = grad_hidden + branch_one

    sums = lax.psum(jnp.stack([sum_one, sum_two]), ("dp", "row", "col"))
    sums = lax.dynamic_slice_in_dim(sums, lax.axis_index("col") * feat, feat, 1)
    return (
        split_rows(result),
        split_rows(grad_tokens.astype(low)).astype(jnp.float32),
        sums[0],
        grad_qkv.reshape(qkv_weight.shape),
        grad_attn,
        sums[1],
        grad_in,
        grad_out,
    )


def solution(mesh):
    return jax.shard_map(
        shards,
        mesh=mesh,
        in_specs=(
            P(("dp", "row"), "col"),
            P("dp"),
            P("col"),
            P("col", None, "row", None),
            P("row", "col"),
            P("col"),
            P("col", None, "row"),
            P("row", "col"),
            P(("dp", "row"), "col"),
        ),
        out_specs=(
            P(("dp", "row"), "col"),
            P(("dp", "row"), "col"),
            P("col"),
            P("col", None, "row", None),
            P("row", "col"),
            P("col"),
            P("col", None, "row"),
            P("row", "col"),
        ),
        check_vma=False,
    )
```

time: 3390 us -> 822 us (0.24)
  waiting for transfers between devices: 2440 us -> 170 us
  matrix products: 374 us -> 139 us
  Pallas kernels: 0 us -> 122 us
  other arithmetic: 150 us -> 43.5 us
  loops' own time: 73.2 us -> 0 us
  local copies, waits for them, and re-layouts: 251 us -> 196 us
    reduce_scatter x8 -> x4, waiting for transfers between devices: 1490 us -> 80.3 us  [sum_plane(): part = lax.psum_scatter(stacked, PLANE, scatter_dimension=0, tiled=False)]
    all_gather x8 -> x4, waiting for transfers between devices: 779 us -> 12.6 us  [gather_plane(): return lax.all_gather(local, PLANE, axis=0, tiled=False)]
    dot_general x68 -> x14, matrix products: 374 us -> 139 us  [the longest x5 57.6 us: dot_nt(): lax.dot_general(left, right, (((1,), (1,)), ((), ())), preferred_element_...]
    dynamic_update_slice x32 -> x0, local copies, waits for them, and re-layouts: 153 us -> none  [the longest x16 96.4 us: attend_back_sequence(): lax.scan(one_block, (zeros_pad, zeros_pad), (offsets, log_totals))]
    psum x1, waiting for transfers between devices: 171 us -> 32.5 us  [sum_plane(): return lax.psum(part, 'dp').astype(jnp.float32)]
    pallas_call x0 -> x2, Pallas kernels: none -> 122 us  [the longest x1 65.3 us: attend(): pl.pallas_call(functools.partial(forward_kernel, count // BLOCK), grid=(p...]
    reshape x1 -> x8, local copies, waits for them, and re-layouts: 5.31 us -> 98.9 us  [the longest x2 27.5 us: out_full(): stack = stack.reshape((rows, cols) + local.shape).transpose(0, 2, 1, 3)]
    another operation x2 -> x0, loops' own time: 73.2 us -> none  [the longest x1 36.9 us: attend_back_sequence(): lax.scan(one_block, (zeros_pad, zeros_pad), (offsets, log_totals))]
  transfers between devices with their start and end apart: 17 -> 17, of which waited for: 17 -> 7; matrix products, arithmetic and copies ran while one was open for 5% -> 32% of each run, Pallas kernels for 0% -> 15%
where the time goes in v1:
time: 822 us; the launch traced here: 811 us
  local copies, waits for them, and re-layouts  196 us (24%)
  waiting for transfers between devices  170 us (21%)
  matrix products  139 us (17%)
  Pallas kernels  122 us (15%)
  blocking collectives  97.2 us (12%)
  other arithmetic  43.5 us (5%)
  starting transfers between devices  28.9 us (4%)
  between operations  14.9 us (2%)
    reduce_scatter x4, waiting for transfers between devices, sum_plane(): part = lax.psum_scatter(stacked, PLANE, scatter_dimension=0, tiled=False)  80.3 us
    pallas_call x1, Pallas kernels, attend(): pl.pallas_call(functools.partial(forward_kernel, count // BLOCK), grid=(p...  65.3 us
    psum x1, blocking collectives, shards(): sums = lax.psum(jnp.stack([sum_one, sum_two]), ('dp', 'row', 'col'))  61.5 us
    dot_general x5, matrix products, dot_nt(): lax.dot_general(left, right, (((1,), (1,)), ((), ())), preferred_element_...  57.6 us
    pallas_call x1, Pallas kernels, attend_back(): pl.pallas_call(functools.partial(backward_kernel, count // BLOCK), grid=(...  56.5 us
    dot_general x5, matrix products, dot_tn(): lax.dot_general(left, right, (((0,), (0,)), ((), ())), preferred_element_...  48.3 us
    all_gather x1, blocking collectives, shards(): lax.all_gather(jnp.stack([norm_one, norm_two]), 'col', axis=1, tiled=True)  35.7 us
    dot_general x4, matrix products, dot_nn(): return jnp.dot(left, right, preferred_element_type=jnp.float32)  33.4 us
  transfers between devices with their start and end apart: 17, of which 7 were waited for; matrix products, arithmetic and copies ran while one was open for 32% of the time, Pallas kernels for 15%

profile of v1, /device:TPU:0, one launch (start us, length us, event | category | flops | bytes accessed | tf_op | source)
XLA Modules:
  0.0 811.5 jit_solution(10398526872248096124)
XLA Ops:
  11.6 4.2 all-to-all-start
  18.9 31.2 %all-to-all-done = bf16[2,1024,512]{2,1,0:T(8,128)(2,1)S(1)} async-done(((bf16[2,1024,512]{2,1,0:T(8,128)(2,1)}), bf16[2,1024,512]{2,1,0:T(8,128)(2,1)S(1)}, u32[]{:S(2)}, u32[]{:S(2)}) %all-to-all-start) | async-done | bytes 2097184 | tf_op jit(solution)/shard_map/all_to_all | solution.py:217
  50.1 4.8 all-to-all-start.1
  55.6 35.7 %all_gather.24 = f32[2,1024]{1,0:T(2,128)S(1)} all-gather(f32[2,512]{1,0:T(2,128)S(1)} %pad_maximum_fusion.2), channel_id=1, replica_groups=mesh['dp'=4,'row'=4,'col'=2] {'col'}, dimensions={1}, use_global_device_ids=true | all-gather | bytes 12288 | tf_op jit(solution)/shard_map/all_gather | solution.py:273
  93.7 4.6 collective-permute-start
  98.3 3.4 copy.111
  106.0 3.8 fusion.6
  109.8 3.7 copy.83
  115.5 23.8 %copy.87 = bf16[4,2,656,512]{3,1,2,0:T(2,128)(2,1)S(1)} copy(bf16[4,2,656,512]{3,2,1,0:T(8,128)(2,1)} %bitcast.143) | data formatting | bytes 10747904 | tf_op jit(solution)/shard_map/reshape | solution.py:265
  139.3 4.1 copy.115
  143.4 12.6 %all-gather.8.cloned.1.call-done = bf16[8,512,3,256]{3,1,2,0:T(8,128)(2,1)} async-done(((bf16[1,512,3,256]{3,1,2,0:T(8,128)(2,1)}), bf16[8,512,3,256]{3,1,2,0:T(8,128)(2,1)}) %all-gather.8.cloned.1.call-update) | async-done | bytes 6291472 | tf_op jit(solution)/shard_map/all_gather | solution.py:225
  156.0 10.6 %copy.80 = bf16[2,512,3,4,256]{4,3,2,1,0:T(4,128)(2,1)} copy(bf16[2,512,3,4,256]{4,1,2,0,3:T(8,128)(2,1)} %bitcast.142) | data formatting | bytes 12582912 | tf_op jit(solution)/shard_map/transpose | solution.py:261
  166.6 11.7 %reshape.246.wq_ref.wk_ref.wv_ref = bf16[1024,3072]{1,0:T(8,128)(2,1)} reshape(bf16[2,512,3,4,256]{4,3,2,1,0:T(4,128)(2,1)} %copy.80) | data formatting | bytes 12582912 | tf_op jit(solution)/shard_map/reshape | solution.py:261
  178.3 65.3 %attend_forward.1 = (bf16[1024,1024]{1,0:T(8,128)(2,1)S(1)}, bf16[1152,1024]{1,0:T(8,128)(2,1)}, bf16[1152,1024]{1,0:T(8,128)(2,1)}, bf16[1024,1024]{1,0:T(8,128)(2,1)}) custom-call(bf16[1152,1024]{1,0:T(8,128)(2,1)} %get-tuple-element.48.normed_ref, bf16[1024,3072]{1,0:T(8,128)(2,1)} %reshape.246.wq_ref.wk_ref.wv_ref, ...), custom_call_target="tpu_custom_call" | custom-call | flops 9395240960 | bytes 18087936 | tf_op jit(solution)/shard_map/attend_forward/pallas_call | solution.py:140
  243.6 4.8 fusion.31
  252.4 19.3 %copy.119 = bf16[4,2,2,656,512]{4,1,3,0,2:T(2,128)(2,1)S(1)} copy(bf16[4,2,2,656,512]{4,3,2,1,0:T(8,128)(2,1)} %bitcast.130) | data formatting | bytes 21495808 | tf_op jit(solution)/shard_map/reshape | solution.py:270
  271.7 7.9 fusion.27
  279.6 4.1 copy.113
  285.4 8.4 %fusion.33 = f32[1024,2624]{0,1:T(8,128)} fusion(bf16[1024,1024]{1,0:T(8,128)(2,1)S(1)} %copy-done.15, bf16[2624,1024]{1,0:T(8,128)(2,1)S(1)} %bitcast.148), kind=kOutput, calls=%fused_computation.104 | convolution fusion | flops 5502926848 | bytes 18219008 | tf_op jit(solution)/shard_map/dot_general | solution.py:28
  293.9 8.6 %fusion.32 = f32[1024,2624]{0,1:T(8,128)} fusion(bf16[1024,1024]{1,0:T(8,128)(2,1)S(1)} %copy-done.15, bf16[2624,1024]{1,0:T(8,128)(2,1)S(1)} %bitcast.153), kind=kOutput, calls=%fused_computation.103 | convolution fusion | flops 5502926848 | bytes 18219008 | tf_op jit(solution)/shard_map/dot_general | solution.py:28
  302.4 17.8 %multiply_convert_fusion = (bf16[1024,2624]{0,1:T(8,128)(2,1)}, bf16[1024,2624]{0,1:T(8,128)(2,1)}, bf16[1024,2624]{0,1:T(8,128)(2,1)}) fusion(f32[1024,2624]{0,1:T(8,128)} %fusion.32, f32[1024,2624]{0,1:T(8,128)} %fusion.33, bf16[1024,1024]{1,0:T(8,128)(2,1)S(1)} %bitcast.134, bf16[2624,1024]{1,0:T(8,128)(2,1)S(1)} %bitcast.147), kind=kOutput, calls=%fused_computation.9 | convolution fusion | flops 5545918464 | bytes 45088768 | tf_op jit(solution)/shard_map/dot_general | solution.py:28
  320.3 10.1 %fusion.34 = f32[1024,1024]{1,0:T(8,128)S(1)} fusion(bf16[1024,2624]{0,1:T(8,128)(2,1)} %get-tuple-element.20, bf16[2624,1024]{1,0:T(8,128)(2,1)} %bitcast.150), kind=kOutput, calls=%fused_computation.105 | convolution fusion | flops 5502926848 | bytes 14942208 | tf_op jit(solution)/shard_map/dot_general | solution.py:24
  330.4 7.9 multiply_reduce_fusion
  342.4 3.8 convolution_convert_fusion.4
  346.1 4.5 reshape.256
  354.0 10.4 %convolution_convert_fusion = bf16[2624,1024]{1,0:T(8,128)(2,1)} fusion(bf16[1024,2624]{0,1:T(8,128)(2,1)} %get-tuple-element.19, bf16[1024,1024]{1,0:T(8,128)(2,1)} %bitcast.133), kind=kOutput, calls=%fused_computation.15 | convolution fusion | flops 5505613824 | bytes 12845056 | tf_op jit(solution)/shard_map/dot_general | solution.py:34
  364.4 13.1 %reshape.259 = bf16[4,656,2,512]{3,2,1,0:T(2,128)(2,1)} reshape(bf16[2624,1024]{1,0:T(8,128)(2,1)} %convolution_convert_fusion) | data formatting | bytes 10747904 | tf_op jit(solution)/shard_map/reshape | solution.py:321
  377.5 5.8 copy.100
  383.4 6.6 convolution_convert_fusion.5.grad_ref
  390.0 56.5 %attend_backward.1 = (bf16[1024,1024]{1,0:T(8,128)(2,1)S(1)}, bf16[1152,1024]{1,0:T(8,128)(2,1)}, bf16[1152,1024]{1,0:T(8,128)(2,1)}) custom-call(bf16[1024,1024]{1,0:T(8,128)(2,1)} %copy-done, bf16[1152,1024]{1,0:T(8,128)(2,1)} %get-tuple-element.23.k_ref, bf16[1152,1024]{1,0:T(8,128)(2,1)} %get-tuple-element.24.v_ref, ...), custom_call_target="tpu_custom_call" | custom-call | flops 6442450944 | bytes 16515072 | tf_op jit(solution)/shard_map/attend_backward/pallas_call | solution.py:173
  454.9 7.5 collective-permute-done.2
  463.7 13.1 %convolution_convert_fusion.3 = bf16[1024,3072]{1,0:T(8,128)(2,1)} fusion(bf16[1152,1024]{1,0:T(8,128)(2,1)S(1)} %copy-done.14, bf16[64,2048]{1,0:T(8,128)(2,1)S(1)} %get-tuple-element.44, bf16[896,2048]{1,0:T(8,128)(2,1)S(1)} %slice.116, bf16[64,2048]{1,0:T(8,128)(2,1)S(1)} %get-tuple-element.43, bf16[1024,1024]{1,0:T(8,128)(2,1)S(1)} %get-tuple-element.25), kind=kOutput, calls=%fused_computation.18 | convolution fusion | flops 6470762496 | bytes 14680064 | tf_op jit(solution)/shard_map/dot_general | solution.py:34
  476.8 12.1 %reshape.252 = bf16[2,512,3,4,256]{4,3,2,1,0:T(4,128)(2,1)} reshape(bf16[1024,3072]{1,0:T(8,128)(2,1)} %convolution_convert_fusion.3) | data formatting | bytes 12582912 | tf_op jit(solution)/shard_map/reshape | solution.py:350
  489.0 10.6 %copy.97 = bf16[2,512,3,4,256]{1,4,2,0,3:T(8,128)(2,1)} copy(bf16[2,512,3,4,256]{4,3,2,1,0:T(4,128)(2,1)} %reshape.252) | data formatting | bytes 12582912 | tf_op jit(solution)/shard_map/reshape | solution.py:350
  501.1 10.3 %convolution_convert_fusion.1 = bf16[2624,1024]{1,0:T(8,128)(2,1)} fusion(bf16[1024,2624]{0,1:T(8,128)(2,1)} %get-tuple-element.21, bf16[1024,1024]{1,0:T(8,128)(2,1)S(1)} %copy-done.16), kind=kOutput, calls=%fused_computation.16 | convolution fusion | flops 5505613824 | bytes 12845056 | tf_op jit(solution)/shard_map/dot_general | solution.py:34
  511.4 13.2 %stack.70 = bf16[1,4,656,2,512]{4,3,2,1,0:T(2,128)(2,1)} reshape(bf16[2624,1024]{1,0:T(8,128)(2,1)} %convolution_convert_fusion.1) | data formatting | bytes 10747904 | tf_op jit(solution)/shard_map/stack | solution.py:325
  524.6 10.8 %convolution_convert_fusion.2 = bf16[2624,1024]{1,0:T(8,128)(2,1)} fusion(bf16[1024,2624]{0,1:T(8,128)(2,1)} %get-tuple-element.20, bf16[1024,1024]{1,0:T(8,128)(2,1)S(1)} %copy-done.16), kind=kOutput, calls=%fused_computation.17 | convolution fusion | flops 5505613824 | bytes 12845056 | tf_op jit(solution)/shard_map/dot_general | solution.py:34
  535.5 13.0 %stack.69 = bf16[1,4,656,2,512]{4,3,2,1,0:T(2,128)(2,1)} reshape(bf16[2624,1024]{1,0:T(8,128)(2,1)} %convolution_convert_fusion.2) | data formatting | bytes 10747904 | tf_op jit(solution)/shard_map/stack | solution.py:325
  548.5 17.5 %maximum_bitcast_fusion = bf16[4,2,2,656,512]{4,1,3,0,2:T(2,128)(2,1)S(1)} fusion(bf16[1,4,656,2,512]{4,3,2,1,0:T(2,128)(2,1)} %stack.70, bf16[1,4,656,2,512]{4,3,2,1,0:T(2,128)(2,1)} %stack.69), kind=kLoop, calls=%fused_computation.7 | loop fusion | flops 5373952 | bytes 21495808 | tf_op jit(solution)/shard_map/transpose | solution.py:326
  566.0 5.4 copy.99
  572.2 10.6 %add_convert_fusion.1 = bf16[1024,1024]{1,0:T(8,128)(2,1)S(1)} fusion(f32[1024,1024]{1,0:T(8,128)} %copy-done.3, bf16[1024,2624]{0,1:T(8,128)(2,1)} %get-tuple-element.19, bf16[2624,1024]{1,0:T(8,128)(2,1)} %bitcast.144), kind=kOutput, calls=%fused_computation.29 | convolution fusion | flops 5505024000 | bytes 17039360 | tf_op jit(solution)/shard_map/dot_general | solution.py:24
  584.3 5.2 all-to-all-start.2
  589.6 80.2 %reduce-scatter.9.cloned.1.call-done = bf16[1,2,656,512]{3,2,1,0:T(8,128)(2,1)} async-done(((bf16[8,2,656,512]{3,2,1,0:T(8,128)(2,1)}), bf16[1,2,656,512]{3,2,1,0:T(8,128)(2,1)}) %reduce-scatter.9.cloned.1.call-update) | async-done | bytes 1343504 | tf_op jit(solution)/shard_map/reduce_scatter | solution.py:229
  669.9 16.2 %multiply_reduce_fusion.1 = (f32[1024]{0:T(1024)S(1)}, f32[1024]{0:T(1024)S(1)}, f32[1024]{0:T(1024)S(1)}, f32[1024,1024]{1,0:T(8,128)}) fusion(f32[1152,1024]{1,0:T(8,128)} %get-tuple-element.47, f32[1024]{0:T(1024)S(1)} %bitcast.172, bf16[1024,3072]{1,0:T(8,128)(2,1)} %reshape.246.wq_ref.wk_ref.wv_ref, bf16[64,2048]{1,0:T(8,128)(2,1)S(1)} %get-tuple-element.44, ...), kind=kOutput, calls=%fused_computation.24 | convolution fusion | flops 6473905152 | bytes 20987904 | tf_op jit(solution)/shard_map/dot_general | solution.py:28
  686.1 4.2 add_convert_fusion
  691.8 3.8 all-to-all-start.3
  695.6 61.5 %psum.35 = f32[2,1024]{1,0:T(2,128)S(1)} all-reduce(f32[2,1024]{1,0:T(2,128)S(1)} %pad_maximum_fusion.1), channel_id=1, replica_groups=mesh['dp'=4,'row'=4,'col'=2] {'dp','row','col'}, use_global_device_ids=true, to_apply=%region_10.11 | all-reduce | flops 2048 | bytes 16384 | tf_op jit(solution)/shard_map/psum | solution.py:358
  760.3 32.5 %all-reduce.4.cloned.1.call-done = (bf16[512,3,4,64]{0,3,2,1:T(8,128)(2,1)}, bf16[256,512]{1,0:T(8,128)(2,1)}, bf16[512,2,656]{0,2,1:T(8,128)(2,1)}, bf16[656,512]{1,0:T(8,128)(2,1)}) async-done(((bf16[512,3,4,64]{0,3,2,1:T(8,128)(2,1)}, bf16[256,512]{1,0:T(8,128)(2,1)}, bf16[512,2,656]{0,2,1:T(8,128)(2,1)}, bf16[656,512]{1,0:T(8,128)(2,1)}), (bf16[512,3,4,64]{0,3,2,1:T(8,128)(2,1)}, ...) | async-done | bytes 3063824 | tf_op jit(solution)/shard_map/psum | solution.py:230
  (150 shorter events, 59.7 us)
Async XLA Ops:
  7.2 102.6 %all-gather.10.cloned.1.call-start = ((), (), s32[]{:S(2)}) async-start(), calls=%async_computation.13 | async-start | bytes 2359296 | tf_op jit(solution)/shard_map/all_gather | solution.py:225
  7.9 107.6 %all-gather.14.cloned.1.call-start = ((), (), s32[]{:S(2)}) async-start(), calls=%async_computation.15 | async-start | bytes 6045696 | tf_op jit(solution)/shard_map/all_gather | solution.py:225
  8.7 147.4 %all-gather.8.cloned.1.call-start = ((), (), s32[]{:S(2)}) async-start(), calls=%async_computation.8 | async-start | bytes 7077888 | tf_op jit(solution)/shard_map/all_gather | solution.py:225
  11.0 241.4 %all-gather.12.cloned.1.call-start = ((), (), s32[]{:S(2)}) async-start(), calls=%async_computation.14 | async-start | bytes 12091392 | tf_op jit(solution)/shard_map/all_gather | solution.py:225
  11.6 38.5 %all-to-all-start = ((bf16[2,1024,512]{2,1,0:T(8,128)(2,1)}), bf16[2,1024,512]{2,1,0:T(8,128)(2,1)S(1)}, u32[]{:S(2)}, u32[]{:S(2)}) async-start(bf16[2,1024,512]{2,1,0:T(8,128)(2,1)} %bitcast.157), calls=%async_computation | async-start | bytes 4194304 | tf_op jit(solution)/shard_map/all_to_all | solution.py:217
  15.8 39.2 %copy-start.23 = (s32[8192]{0:T(1024)S(1)}, s32[8192]{0:T(1024)}, u32[]{:S(2)}) copy-start(s32[8192]{0:T(1024)} %param.10) | copy-start | bytes 98308
  16.5 39.1 %copy-start.24 = (f32[512]{0:T(512)S(1)}, f32[512]{0:T(512)}, u32[]{:S(2)}) copy-start(f32[512]{0:T(512)} %param.14) | copy-start | bytes 6148
  16.5 39.1 %copy-start.25 = (f32[512]{0:T(512)S(1)}, f32[512]{0:T(512)}, u32[]{:S(2)}) copy-start(f32[512]{0:T(512)} %param.11) | copy-start | bytes 6148
  50.1 5.2 copy-start.9
  50.1 48.1 %all-to-all-start.1 = ((bf16[2,1024,512]{2,1,0:T(8,128)(2,1)}), bf16[2,1024,512]{2,1,0:T(8,128)(2,1)}, u32[]{:S(2)}, u32[]{:S(2)}) async-start(bf16[2,1024,512]{2,1,0:T(8,128)(2,1)} %bitcast.158), calls=%async_computation.1 | async-start | bytes 4194304 | tf_op jit(solution)/shard_map/all_to_all | solution.py:217
  54.9 534.6 %reduce-scatter.7.cloned.1.call-start = ((), (), s32[]{:S(2)}) async-start(), calls=%async_computation.10 | async-start | bytes 2359296 | tf_op jit(solution)/shard_map/reduce_scatter | solution.py:229
  92.4 9.6 %collective-permute-start.1 = (bf16[64,1024]{1,0:T(8,128)(2,1)S(1)}, bf16[64,1024]{1,0:T(8,128)(2,1)S(1)}, u32[]{:S(2)}, u32[]{:S(2)}) collective-permute-start(bf16[64,1024]{1,0:T(8,128)(2,1)S(1)} %bitcast.170), channel_id=1, source_target_pairs={{1,0},{2,1},{3,2},{4,3},{5,4},{6,5},{7,6},{9,8},{10,9},{11,10},{12... | collective-permute-start | bytes 393224 | tf_op jit(solution)/shard_map/ppermute | solution.py:281
  93.7 10.6 %collective-permute-start = (bf16[64,1024]{1,0:T(8,128)(2,1)S(1)}, bf16[64,1024]{1,0:T(8,128)(2,1)S(1)}, u32[]{:S(2)}, u32[]{:S(2)}) collective-permute-start(bf16[64,1024]{1,0:T(8,128)(2,1)S(1)} %bitcast.169), channel_id=1, source_target_pairs={{0,1},{1,2},{2,3},{3,4},{4,5},{5,6},{6,7},{8,9},{9,10},{10,11},{11... | collective-permute-start | bytes 393224 | tf_op jit(solution)/shard_map/ppermute | solution.py:280
  98.2 7.2 copy-start.21
  98.3 3.4 copy-start.10
  102.0 3.5 copy-start.5
  178.3 65.3 %copy-start.6 = (bf16[2,128,8,512]{3,2,0,1:T(8,128)(2,1)S(1)}, bf16[2,128,8,512]{3,2,0,1:T(8,128)(2,1)}, u32[]{:S(2)}) copy-start(bf16[2,128,8,512]{3,2,0,1:T(8,128)(2,1)} %copy-done.5) | copy-start | bytes 6291460
  178.3 65.3 %copy-start.17 = (bf16[128,8,2,512]{3,1,2,0:T(8,128)(2,1)S(1)}, bf16[128,8,2,512]{3,1,2,0:T(8,128)(2,1)}, u32[]{:S(2)}) copy-start(bf16[128,8,2,512]{3,1,2,0:T(8,128)(2,1)} %copy.112) | copy-start | bytes 6291460
  243.6 4.8 copy-start
  248.4 2.0 copy-start.3
  283.7 1.7 copy-start.15
  283.7 10.2 %slice-start.2 = ((s8[5373952]{0:T(1024)(128)(4,1)}), s8[1179648]{0:T(1024)(128)(4,1)S(1)}, s32[]{:S(2)}) async-start(s8[5373952]{0:T(1024)(128)(4,1)} %bitcast.151), calls=%async_computation.19 | async-start | bytes 2359296
  285.4 8.4 %slice-start.3 = ((s8[5373952]{0:T(1024)(128)(4,1)}), s8[4194304]{0:T(1024)(128)(4,1)S(1)}, s32[]{:S(2)}) async-start(s8[5373952]{0:T(1024)(128)(4,1)} %bitcast.151), calls=%async_computation.20 | async-start | bytes 8388608
  285.4 17.0 %slice-start = ((s8[5373952]{0:T(1024)(128)(4,1)}), s8[4194304]{0:T(1024)(128)(4,1)S(1)}, s32[]{:S(2)}) async-start(s8[5373952]{0:T(1024)(128)(4,1)} %bitcast.145), calls=%async_computation.17 | async-start | bytes 8388608
  293.8 8.6 %copy-start.11 = (bf16[2,128,8,512]{3,2,0,1:T(8,128)(2,1)S(1)}, bf16[2,128,8,512]{3,2,0,1:T(8,128)(2,1)}, u32[]{:S(2)}) copy-start(bf16[2,128,8,512]{3,2,0,1:T(8,128)(2,1)} %copy.111) | copy-start | bytes 6291460
  293.8 8.6 %slice-start.1 = ((s8[5373952]{0:T(1024)(128)(4,1)}), s8[1179648]{0:T(1024)(128)(4,1)S(1)}, s32[]{:S(2)}) async-start(s8[5373952]{0:T(1024)(128)(4,1)} %bitcast.145), calls=%async_computation.18 | async-start | bytes 2359296
  320.3 10.1 %copy-start.4 = (f32[1024,1024]{1,0:T(8,128)S(1)}, f32[1024,1024]{1,0:T(8,128)}, u32[]{:S(2)}) copy-start(f32[1024,1024]{1,0:T(8,128)} %copy-done.3) | copy-start | bytes 12582916
  320.3 10.1 %copy-start.26 = (bf16[1024,2624]{0,1:T(8,128)(2,1)S(1)}, bf16[1024,2624]{0,1:T(8,128)(2,1)}, u32[]{:S(2)}) copy-start(bf16[1024,2624]{0,1:T(8,128)(2,1)} %get-tuple-element.21) | copy-start | bytes 16121860
  338.3 4.0 copy-start.27
  340.4 2.0 copy-start.7
  354.0 235.6 %reduce-scatter.11.cloned.1.call-start = ((), (), s32[]{:S(2)}) async-start(), calls=%async_computation.12 | async-start | bytes 6045696 | tf_op jit(solution)/shard_map/reduce_scatter | solution.py:229
  383.3 206.3 %reduce-scatter.5.cloned.1.call-start = ((), (), s32[]{:S(2)}) async-start(), calls=%async_computation.9 | async-start | bytes 7077888 | tf_op jit(solution)/shard_map/reduce_scatter | solution.py:229
  446.4 17.3 %copy-start.1 = (bf16[1024,1024]{1,0:T(8,128)(2,1)}, bf16[1024,1024]{1,0:T(8,128)(2,1)S(1)}, u32[]{:S(2)}) copy-start(bf16[1024,1024]{1,0:T(8,128)(2,1)S(1)} %get-tuple-element.25) | copy-start | bytes 6291460
  446.4 3.1 copy-start.13
  449.8 12.6 %collective-permute-start.2 = (bf16[64,2048]{1,0:T(8,128)(2,1)S(1)}, bf16[64,2048]{1,0:T(8,128)(2,1)S(1)}, u32[]{:S(2)}, u32[]{:S(2)}) collective-permute-start(bf16[64,2048]{1,0:T(8,128)(2,1)S(1)} %get-tuple-element.45), channel_id=1, source_target_pairs={{0,1},{1,2},{2,3},{3,4},{4,5},{5,6},{6,7},{8,9},{9,10},{10,11},{11... | collective-permute-start | bytes 786440 | tf_op jit(solution)/shard_map/ppermute | solution.py:337
  453.0 10.7 %copy-start.14 = (bf16[1152,1024]{1,0:T(8,128)(2,1)S(1)}, bf16[1152,1024]{1,0:T(8,128)(2,1)}, u32[]{:S(2)}) copy-start(bf16[1152,1024]{1,0:T(8,128)(2,1)} %get-tuple-element.48.normed_ref) | copy-start | bytes 7077892
  453.0 10.6 %collective-permute-start.3 = (bf16[64,2048]{1,0:T(8,128)(2,1)S(1)}, bf16[64,2048]{1,0:T(8,128)(2,1)S(1)}, u32[]{:S(2)}, u32[]{:S(2)}) collective-permute-start(bf16[64,2048]{1,0:T(8,128)(2,1)S(1)} %get-tuple-element.46), channel_id=1, source_target_pairs={{1,0},{2,1},{3,2},{4,3},{5,4},{6,5},{7,6},{9,8},{10,9},{11,10},{12... | collective-permute-start | bytes 786440 | tf_op jit(solution)/shard_map/ppermute | solution.py:338
  454.9 8.8 %copy-start.12 = (bf16[896,2048]{1,0:T(8,128)(2,1)}, bf16[896,2048]{1,0:T(8,128)(2,1)S(1)}, u32[]{:S(2)}) copy-start(bf16[896,2048]{1,0:T(8,128)(2,1)S(1)} %slice.116) | copy-start | bytes 11010052
  499.5 1.6 copy-start.16
  499.6 170.3 %reduce-scatter.9.cloned.1.call-start = ((), (), s32[]{:S(2)}) async-start(), calls=%async_computation.11 | async-start | bytes 12091392 | tf_op jit(solution)/shard_map/reduce_scatter | solution.py:229
  571.4 0.7 copy-start.20
  584.3 85.6 %copy-start.2 = (bf16[1024,1024]{1,0:T(8,128)(2,1)S(1)}, bf16[1024,1024]{1,0:T(8,128)(2,1)}, u32[]{:S(2)}) copy-start(bf16[1024,1024]{1,0:T(8,128)(2,1)} %copy-done.1) | copy-start | bytes 6291460
  584.3 85.7 %copy-start.22 = (f32[1,1024]{1,0:T(1,128)S(1)}, f32[1,1024]{1,0:T(1,128)}, u32[]{:S(2)}) copy-start(f32[1,1024]{1,0:T(1,128)} %copy-done.21) | copy-start | bytes 12292
  584.3 107.5 %all-to-all-start.2 = ((bf16[1024,2,512]{2,0,1:T(8,128)(2,1)}), bf16[1024,2,512]{2,0,1:T(8,128)(2,1)}, u32[]{:S(2)}, u32[]{:S(2)}) async-start(bf16[1024,2,512]{2,0,1:T(8,128)(2,1)} %bitcast.137), calls=%async_computation.2 | async-start | bytes 4194304 | tf_op jit(solution)/shard_map/all_to_all | solution.py:221
  589.5 203.3 %all-reduce.4.cloned.1.call-start = ((), (), s32[]{:S(2)}) async-start(), calls=%async_computation.16 | async-start | bytes 6127616 | tf_op jit(solution)/shard_map/psum | solution.py:230
  669.9 16.2 %copy-start.8 = (f32[1024,1024]{1,0:T(8,128)S(1)}, f32[1024,1024]{1,0:T(8,128)}, u32[]{:S(2)}) copy-start(f32[1024,1024]{1,0:T(8,128)} %copy-done.7) | copy-start | bytes 12582916
  691.8 65.9 %all-to-all-start.3 = ((bf16[1024,2,512]{2,0,1:T(8,128)(2,1)}), bf16[1024,2,512]{2,0,1:T(8,128)(2,1)S(1)}, u32[]{:S(2)}, u32[]{:S(2)}) async-start(bf16[1024,2,512]{2,0,1:T(8,128)(2,1)} %bitcast.138), calls=%async_computation.3 | async-start | bytes 4194304 | tf_op jit(solution)/shard_map/all_to_all | solution.py:221
  792.8 6.7 copy-start.18
  (1 other events, 0.6 us)
Sparse Core Ops, SparseCore 0:
  9.9 39.2 all-gather.9
  51.1 55.6 all-gather.13
  109.2 46.7 all-gather.7
  157.8 64.5 all-gather.11
  354.1 41.3 reduce-scatter.6
  399.1 57.2 reduce-scatter.10
  499.7 64.6 reduce-scatter.4
  571.5 98.2 reduce-scatter.8
  672.7 120.0 all-reduce.3

commit v2 on v1

v2 whole, which is shorter than its diff:
```python
import functools

import jax
import jax.numpy as jnp
from jax import lax
from jax.experimental import pallas as pl
from jax.experimental.pallas import tpu as pltpu
from jax.sharding import PartitionSpec as P

WINDOW = 128
HALF = WINDOW // 2
SEQ = 4096
BLOCK = 128
PAIR = 128
LANES = 256

EPS = 1e-05
NEG = -1e30
THETA = 10000.0
PLANE = ("x", "core", "col")
CHIPS = ("x", "col")
VMEM_LIMIT = 48 * 1024 * 1024


def dot_nn(left, right):
    return jnp.dot(left, right, preferred_element_type=jnp.float32)


def dot_nt(left, right):
    return lax.dot_general(
        left, right, (((1,), (1,)), ((), ())), preferred_element_type=jnp.float32
    )


def dot_tn(left, right):
    return lax.dot_general(
        left, right, (((0,), (0,)), ((), ())), preferred_element_type=jnp.float32
    )


def first_half(shape):
    return lax.broadcasted_iota(jnp.int32, shape, 1) % 64 < 32


def turn(values_in):
    ahead = pltpu.roll(values_in, values_in.shape[1] - 32, 1)
    behind = pltpu.roll(values_in, 32, 1)
    return jnp.where(first_half(values_in.shape), -ahead, behind)


def turn_back(values_in):
    ahead = pltpu.roll(values_in, values_in.shape[1] - 32, 1)
    behind = pltpu.roll(values_in, 32, 1)
    return jnp.where(first_half(values_in.shape), ahead, -behind)


def forward_kernel(
    blocks, normed_ref, wq_ref, wk_ref, wv_ref, cos_ref, sin_ref, bias_ref, q_ref, k_ref, v_ref, mix_ref
):
    cos_tab = cos_ref[...]
    sin_tab = sin_ref[...]
    own = pl.ds(HALF, blocks * BLOCK)
    queries = dot_nt(normed_ref[own, :], wq_ref[0, 0])
    queries = queries * cos_tab[HALF:-HALF] + turn(queries) * sin_tab[HALF:-HALF]
    q_ref[...] = queries.astype(jnp.bfloat16) * jnp.bfloat16(0.125)
    keys = dot_nt(normed_ref[...], wk_ref[0, 0])
    keys = keys * cos_tab + turn(keys) * sin_tab
    k_ref[...] = keys.astype(jnp.bfloat16)
    v_ref[...] = dot_nt(normed_ref[...], wv_ref[0, 0]).astype(jnp.bfloat16)
    lower = lax.broadcasted_iota(jnp.int32, (BLOCK, PAIR), 1) < 64
    for block in range(blocks):
        rows = pl.ds(block * BLOCK, BLOCK)
        span = pl.ds(block * BLOCK, BLOCK + WINDOW)
        bias = bias_ref[rows, :]
        for pair in range(LANES // PAIR):
            lanes = pl.ds(pair * PAIR, PAIR)
            q_blk = q_ref[rows, lanes]
            k_blk = k_ref[span, lanes]
            v_blk = v_ref[span, lanes]
            outs = []
            for head in range(2):
                q_head = jnp.where(lower if head == 0 else ~lower, q_blk, jnp.bfloat16(0))
                scores = dot_nt(q_head, k_blk) + bias
                weights = jnp.exp(scores - jnp.max(scores, -1, keepdims=True))
                probs = weights * (1.0 / jnp.sum(weights, -1, keepdims=True))
                outs.append(dot_nn(probs.astype(jnp.bfloat16), v_blk))
            mix_ref[rows, lanes] = jnp.where(lower, outs[0], outs[1]).astype(jnp.bfloat16)


def backward_kernel(
    blocks, q_ref, k_ref, v_ref, grad_ref, cos_ref, sin_ref, bias_ref, dq_ref, dk_ref, dv_ref, dk_acc, dv_acc
):
    dk_acc[...] = jnp.zeros_like(dk_acc)
    dv_acc[...] = jnp.zeros_like(dv_acc)
    lower = lax.broadcasted_iota(jnp.int32, (BLOCK, PAIR), 1) < 64
    for block in range(blocks):
        rows = pl.ds(block * BLOCK, BLOCK)
        span = pl.ds(block * BLOCK, BLOCK + WINDOW)
        own = pl.ds(block * BLOCK + HALF, BLOCK)
        bias = bias_ref[rows, :]
        for pair in range(LANES // PAIR):
            lanes = pl.ds(pair * PAIR, PAIR)
            q_blk = q_ref[rows, lanes]
            k_blk = k_ref[span, lanes]
            v_blk = v_ref[span, lanes]
            g_blk = grad_ref[rows, lanes]
            dq_parts = []
            dk_part = 0.0
            dv_part = 0.0
            for head in range(2):
                mask = lower if head == 0 else ~lower
                q_head = jnp.where(mask, q_blk, jnp.bfloat16(0))
                g_head = jnp.where(mask, g_blk, jnp.bfloat16(0))
                scores = dot_nt(q_head, k_blk) + bias
                weights = jnp.exp(scores - jnp.max(scores, -1, keepdims=True))
                probs = weights * (1.0 / jnp.sum(weights, -1, keepdims=True))
                grad_probs = dot_nt(g_head, v_blk)
                centre = jnp.sum(grad_probs * probs, -1, keepdims=True)
                grad_scores = (probs * (grad_probs - centre)).astype(jnp.bfloat16)
                dq_parts.append(dot_nn(grad_scores, k_blk))
                dk_part += dot_tn(grad_scores, q_head)
                dv_part += dot_tn(probs.astype(jnp.bfloat16), g_head)
            dk_acc[span, lanes] += dk_part
            dv_acc[span, lanes] += dv_part
            dq = jnp.where(lower, dq_parts[0], dq_parts[1]) * 0.125
            dq = dq * cos_ref[own, lanes] + turn_back(dq * sin_ref[own, lanes])
            dq_ref[rows, lanes] = dq.astype(jnp.bfloat16)
    dk = dk_acc[...]
    dk_ref[...] = (dk * cos_ref[...] + turn_back(dk * sin_ref[...])).astype(jnp.bfloat16)
    dv_ref[...] = dv_acc[...].astype(jnp.bfloat16)


def column_block(rows):
    return pl.BlockSpec((rows, LANES), lambda group: (0, group))


def weight_block(width, which):
    return pl.BlockSpec((1, 1, LANES, width), lambda group: (group, which, 0, 0))


def whole_block(shape):
    return pl.BlockSpec(shape, lambda group: (0,) * len(shape))


def attend(normed_ext, qkv_full, cos_tab, sin_tab, bias):
    ext, width = normed_ext.shape
    count = ext - 2 * HALF
    kind = jnp.bfloat16
    return pl.pallas_call(
        functools.partial(forward_kernel, count // BLOCK),
        grid=(width // LANES,),
        in_specs=[
            whole_block(normed_ext.shape),
            weight_block(width, 0),
            weight_block(width, 1),
            weight_block(width, 2),
            whole_block(cos_tab.shape),
            whole_block(sin_tab.shape),
            whole_block(bias.shape),
        ],
        out_specs=[column_block(count), column_block(ext), column_block(ext), column_block(count)],
        out_shape=[
            jax.ShapeDtypeStruct((count, width), kind),
            jax.ShapeDtypeStruct((ext, width), kind),
            jax.ShapeDtypeStruct((ext, width), kind),
            jax.ShapeDtypeStruct((count, width), kind),
        ],
        compiler_params=pltpu.CompilerParams(vmem_limit_bytes=VMEM_LIMIT),
        cost_estimate=pl.CostEstimate(
            flops=2 * ext * width * 3 * width + 4 * count * 256 * 128 * 16,
            bytes_accessed=2 * (3 * width * width + 5 * ext * width),
            transcendentals=count * 256 * 16,
        ),
        name="attend_forward",
    )(normed_ext, qkv_full, qkv_full, qkv_full, cos_tab, sin_tab, bias)


def attend_back(queries, keys, values, grad_mixture, cos_tab, sin_tab, bias):
    ext, width = keys.shape
    count = ext - 2 * HALF
    kind = jnp.bfloat16
    return pl.pallas_call(
        functools.partial(backward_kernel, count // BLOCK),
        grid=(width // LANES,),
        in_specs=[
            column_block(count),
            column_block(ext),
            column_block(ext),
            column_block(count),
            whole_block(cos_tab.shape),
            whole_block(sin_tab.shape),
            whole_block(bias.shape),
        ],
        out_specs=[column_block(count), column_block(ext), column_block(ext)],
        out_shape=[
            jax.ShapeDtypeStruct((count, width), kind),
            jax.ShapeDtypeStruct((ext, width), kind),
            jax.ShapeDtypeStruct((ext, width), kind),
        ],
        scratch_shapes=[pltpu.VMEM((ext, LANES), jnp.float32), pltpu.VMEM((ext, LANES), jnp.float32)],
        compiler_params=pltpu.CompilerParams(vmem_limit_bytes=VMEM_LIMIT),
        cost_estimate=pl.CostEstimate(
            flops=12 * count * 256 * 128 * 16,
            bytes_accessed=2 * 7 * ext * width,
            transcendentals=count * 256 * 16,
        ),
        name="attend_backward",
    )(queries, keys, values, grad_mixture, cos_tab, sin_tab, bias)


def unit_rows(inputs):
    average = jnp.mean(inputs, 1, keepdims=True)
    centred = inputs - average
    inverse_std = lax.rsqrt(jnp.mean(centred * centred, 1, keepdims=True) + EPS)
    return centred * inverse_std, inverse_std


def norm_backward(grad_normed, unit, inverse_std, gain_vec):
    scaled = grad_normed * gain_vec
    average = jnp.mean(scaled, 1, keepdims=True)
    cross = jnp.mean(scaled * unit, 1, keepdims=True)
    return inverse_std * (scaled - average - unit * cross), jnp.sum(grad_normed * unit, 0)


def swap(array_in, axis):
    return lax.ppermute(array_in, axis, [(0, 1), (1, 0)])


def in_order(mine, other):
    first = lax.axis_index("col") == 0
    return jnp.where(first, mine, other), jnp.where(first, other, mine)


def whole_rows(array_in):
    low_rows, high_rows = jnp.split(array_in, 2, 0)
    mine, theirs = in_order(low_rows, high_rows)
    return jnp.concatenate(in_order(mine, swap(theirs, "col")), 1)


def split_rows(array_in):
    low_cols, high_cols = jnp.split(array_in, 2, 1)
    mine, theirs = in_order(low_cols, high_cols)
    return jnp.concatenate(in_order(mine, swap(theirs, "col")), 0)


def gather_plane(local):
    stack = lax.all_gather(local, CHIPS, axis=0, tiled=False)
    cols = lax.axis_size("col")

    def joined(blocks):
        blocks = blocks.reshape((-1, cols) + local.shape)
        return jnp.concatenate([blocks[:, c] for c in range(cols)], -1)

    return joined(stack), joined(swap(stack, "core"))


def other_core(edge):
    parts = jnp.split(edge, 4, 1)
    return jnp.concatenate([parts[1], parts[0], parts[3], parts[2]], 1)


def core_sum(grad, extra=None):
    mine, theirs = jnp.split(grad, 2, 0)
    if extra is not None:
        mine, theirs = jnp.concatenate([mine, extra], 0), jnp.concatenate([theirs, extra], 0)
    arrived = swap(theirs, "core")
    return (mine.astype(jnp.float32) + arrived.astype(jnp.float32)).astype(jnp.bfloat16)


def chip_stack(parts, feat):
    count = lax.axis_size("x")
    cols = lax.axis_size("col")
    stacked = []
    for x in range(count):
        for c in range(cols):
            lanes = slice(c * feat, (c + 1) * feat)
            pieces = []
            for part, shared in parts:
                block = part.shape[0] if shared else part.shape[0] // count
                start = 0 if shared else x * block
                pieces.append(part[start : start + block, lanes])
            stacked.append(jnp.concatenate(pieces, 0))
    return jnp.stack(stacked)


def scatter(stacked):
    return lax.psum_scatter(stacked, CHIPS, scatter_dimension=0, tiled=False)


def gelu_parts(pre):
    cdf = 0.5 * (1.0 + lax.erf(pre * 0.7071067811865476))
    slope = cdf + pre * jnp.exp(-0.5 * pre * pre) * 0.3989422804014327
    return pre * cdf, slope


def shards(
    tokens,
    segment_ids,
    norm_one,
    qkv_weight,
    attn_out_weight,
    norm_two,
    in_weight,
    out_weight,
    cotangent,
):
    cols = lax.axis_size("col")
    plane = lax.axis_size("x") * lax.axis_size("core") * cols
    place = lax.axis_index(PLANE)
    feat = tokens.shape[1]
    width = feat * cols
    heads_width = qkv_weight.shape[2] * qkv_weight.shape[3]
    hidden = in_weight.shape[2]
    low = jnp.bfloat16

    own_tokens = whole_rows(tokens)
    gains = jnp.stack([norm_one, norm_two])
    gain_one, gain_two = jnp.concatenate(in_order(gains, swap(gains, "col")), 1)
    count = own_tokens.shape[0]
    ahead = [(i, i + 1) for i in range(plane - 1)]
    behind = [(i + 1, i) for i in range(plane - 1)]
    before_rows = lax.ppermute(own_tokens[-HALF:], PLANE, ahead)
    after_rows = lax.ppermute(own_tokens[:HALF], PLANE, behind)
    residual_ext = jnp.concatenate([before_rows, own_tokens, after_rows], 0).astype(jnp.float32)
    unit_ext, inverse_ext = unit_rows(residual_ext)
    normed_ext = (unit_ext * gain_one).astype(low)
    normed_one = normed_ext[HALF:-HALF]

    total = segment_ids.shape[0]
    marks = segment_ids + 16 * (lax.iota(jnp.int32, total) // SEQ)
    marks = jnp.pad(marks, (HALF, HALF), constant_values=-1)
    marks = lax.dynamic_slice_in_dim(marks, place * count, count + 2 * HALF, 0)
    blocks = count // BLOCK
    key_marks = jnp.stack([marks[i * BLOCK : i * BLOCK + BLOCK + WINDOW] for i in range(blocks)])
    query_marks = marks[HALF:-HALF].reshape(blocks, BLOCK)
    shape = (BLOCK, BLOCK + WINDOW)
    distance = lax.broadcasted_iota(jnp.int32, shape, 1) - lax.broadcasted_iota(jnp.int32, shape, 0)
    near = jnp.abs(distance - HALF) <= HALF
    allowed = (query_marks[:, :, None] == key_marks[:, None, :]) & near[None]
    bias = jnp.where(allowed, 0.0, NEG).astype(jnp.float32).reshape(count, BLOCK + WINDOW)

    places = (place * count - HALF + lax.iota(jnp.int32, count + 2 * HALF)) % SEQ
    frequencies = THETA ** (-jnp.arange(32, dtype=jnp.float32) * 2.0 / 64)
    angles = places.astype(jnp.float32)[:, None] * frequencies[None, :]
    cos_tab = jnp.tile(jnp.cos(angles), (1, LANES // 32))
    sin_tab = jnp.tile(jnp.sin(angles), (1, LANES // 32))

    qkv_full = jnp.concatenate(gather_plane(qkv_weight.reshape(feat, 3 * heads_width).T), 0)
    qkv_full = qkv_full.reshape(-1, 3, heads_width, width)
    attn_full = jnp.concatenate(gather_plane(attn_out_weight), 0).reshape(width, width)
    in_blocks = gather_plane(in_weight.transpose(1, 2, 0).reshape(2 * hidden, feat))
    input_full = jnp.concatenate([part[:, :hidden] for part in in_blocks], 0).reshape(-1, width)
    gate_full = jnp.concatenate([part[:, hidden:] for part in in_blocks], 0).reshape(-1, width)
    out_full = jnp.concatenate(gather_plane(out_weight), 0).reshape(-1, width)
    own_cotangent = whole_rows(cotangent)

    queries, keys, values, mixture = attend(normed_ext, qkv_full, cos_tab, sin_tab, bias)
    hidden_rows = own_tokens.astype(jnp.float32) + dot_nn(mixture, attn_full)
    unit_two, inverse_two = unit_rows(hidden_rows)
    normed_two = (unit_two * gain_two).astype(low)
    input_half = dot_nt(normed_two, input_full)
    gate_half = dot_nt(normed_two, gate_full)
    grad_active = dot_nt(own_cotangent, out_full)
    gelu, slope = gelu_parts(input_half)
    active = (gelu * gate_half).astype(low)
    grad_input = (grad_active * gate_half * slope).astype(low)
    grad_gate = (grad_active * gelu).astype(low)
    active, grad_input, grad_gate = lax.optimization_barrier((active, grad_input, grad_gate))

    grad_out = core_sum(dot_tn(active, own_cotangent).astype(low))
    out_part = scatter(chip_stack([(grad_out, False)], feat))
    grad_input_weight = core_sum(dot_tn(grad_input, normed_two).astype(low))
    grad_gate_weight = core_sum(dot_tn(grad_gate, normed_two).astype(low))
    in_stack = chip_stack([(grad_input_weight, False), (grad_gate_weight, False)], feat)
    in_stack, grad_input, grad_gate = lax.optimization_barrier((in_stack, grad_input, grad_gate))
    in_part = scatter(in_stack)
    grad_normed_two = dot_nn(grad_input, input_full) + dot_nn(grad_gate, gate_full)
    branch_two, sum_two = norm_backward(grad_normed_two, unit_two, inverse_two, gain_two)
    grad_hidden = own_cotangent.astype(jnp.float32) + branch_two
    grad_branch = grad_hidden.astype(low)
    result = split_rows((hidden_rows + dot_nn(active, out_full)).astype(low))

    grad_mixture = dot_nt(grad_branch, attn_full).astype(low)
    dq, dk_ext, dv_ext = attend_back(queries, keys, values, grad_mixture, cos_tab, sin_tab, bias)
    edges = jnp.concatenate([dk_ext, dv_ext], 1)
    to_next = lax.ppermute(edges[-HALF:], PLANE, ahead)
    to_prev = lax.ppermute(edges[:HALF], PLANE, behind)
    col = lax.axis_index("col")
    to_next = jnp.where(col == 0, other_core(to_next), to_next)
    to_prev = jnp.where(col == cols - 1, other_core(to_prev), to_prev)
    grad_attn = core_sum(dot_tn(mixture, grad_branch).astype(low))
    middle = edges[HALF:-HALF]
    middle = jnp.concatenate(
        [
            (middle[:HALF].astype(jnp.float32) + to_next.astype(jnp.float32)).astype(low),
            middle[HALF:-HALF],
            (middle[-HALF:].astype(jnp.float32) + to_prev.astype(jnp.float32)).astype(low),
        ],
        0,
    )
    pieces = []
    for start in range(0, width, heads_width):
        for part, first in ((dq, 0), (middle, 0), (middle, width)):
            pieces.append(part[:, first + start : first + start + heads_width])
    grad_joined = lax.optimization_barrier(jnp.concatenate(pieces, 1))
    grad_normed_one = dot_nn(grad_joined, qkv_full.reshape(-1, width))
    branch_one, sum_one = norm_backward(
        grad_normed_one, unit_ext[HALF:-HALF], inverse_ext[HALF:-HALF], gain_one
    )
    grad_tokens = split_rows((grad_hidden + branch_one).astype(low)).astype(jnp.float32)

    sums = jnp.pad(jnp.stack([sum_one, sum_two]).astype(low), ((0, 14), (0, 0)))
    grad_qkv = core_sum(dot_tn(grad_joined, normed_one).astype(low), sums)
    heads_rows = grad_qkv.shape[0] - 16
    late_stack = chip_stack(
        [(grad_qkv[:heads_rows], False), (grad_qkv[heads_rows:], True), (grad_attn, False)], feat
    )
    out_sum, in_sum = lax.psum((out_part, in_part), "dp")
    late_stack, out_sum, in_sum = lax.optimization_barrier((late_stack, out_sum, in_sum))
    late_sum = lax.psum(scatter(late_stack), "dp").astype(jnp.float32)
    qkv_rows = 3 * heads_width
    return (
        result,
        grad_tokens,
        late_sum[qkv_rows],
        late_sum[:qkv_rows].T.reshape(qkv_weight.shape),
        late_sum[qkv_rows + 16 :],
        late_sum[qkv_rows + 1],
        in_sum.astype(jnp.float32).reshape(2, hidden, feat).transpose(2, 0, 1),
        out_sum.astype(jnp.float32),
    )


def solution(mesh):
    dp, row, col = (mesh.shape[name] for name in ("dp", "row", "col"))
    devices = mesh.devices.reshape(dp, row // 2, 2, col)
    fine = jax.sharding.Mesh(devices, ("dp", "x", "core", "col"))
    row = ("x", "core")
    rows = ("dp", "x", "core")
    return jax.shard_map(
        shards,
        mesh=fine,
        in_specs=(
            P(rows, "col"),
            P("dp"),
            P("col"),
            P("col", None, row, None),
            P(row, "col"),
            P("col"),
            P("col", None, row),
            P(row, "col"),
            P(rows, "col"),
        ),
        out_specs=(
            P(rows, "col"),
            P(rows, "col"),
            P("col"),
            P("col", None, row, None),
            P(row, "col"),
            P("col"),
            P("col", None, row),
            P(row, "col"),
        ),
        check_vma=False,
    )
```

time: 822 us -> 771 us (0.938)
  waiting for transfers between devices: 170 us -> 382 us
  local copies, waits for them, and re-layouts: 196 us -> 58.5 us
  blocking collectives: 97.2 us -> 0 us
  other arithmetic: 43.5 us -> 79.4 us
  Pallas kernels: 122 us -> 94.7 us
  matrix products: 139 us -> 117 us
  starting transfers between devices: 28.9 us -> 20.2 us
    ppermute x0 -> x14, waiting for transfers between devices: none -> 99.4 us  [swap(): return lax.ppermute(array_in, axis, [(0, 1), (1, 0)])]
    reshape x8 -> x0, local copies, waits for them, and re-layouts: 98.9 us -> none  [the longest x2 27.5 us: out_full(): stack = stack.reshape((rows, cols) + local.shape).transpose(0, 2, 1, 3)]
    psum x1 -> x2, waiting for transfers between devices: 32.5 us -> 127 us  [the longest x1 81.8 us: shards(): out_sum, in_sum = lax.psum((out_part, in_part), 'dp')]
    all_gather x4, waiting for transfers between devices: 12.6 us -> 99.7 us  [gather_plane(): stack = lax.all_gather(local, CHIPS, axis=0, tiled=False)]
    reduce_scatter x4 -> x0, waiting for transfers between devices: 80.3 us -> none  [sum_plane(): part = lax.psum_scatter(stacked, PLANE, scatter_dimension=0, tiled=False)]
    psum x1 -> x0, blocking collectives: 61.5 us -> none  [shards(): sums = lax.psum(jnp.stack([sum_one, sum_two]), ('dp', 'row', 'col'))]
    unnamed x9 -> x12, waiting for transfers between devices: 2 us -> 47.8 us
    all_gather x1 -> x0, blocking collectives: 35.7 us -> none  [shards(): lax.all_gather(jnp.stack([norm_one, norm_two]), 'col', axis=1, tiled=True)]
  transfers between devices with their start and end apart: 17 -> 27, of which waited for: 7 -> 13; matrix products, arithmetic and copies ran while one was open for 32% -> 24% of each run, Pallas kernels for 15% -> 12%
where the time goes in v2:
time: 771 us; the launch traced here: 767 us
  waiting for transfers between devices  382 us (50%)
  matrix products  117 us (15%)
  Pallas kernels  94.7 us (12%)
  other arithmetic  79.4 us (10%)
  local copies, waits for them, and re-layouts  58.5 us (8%)
  starting transfers between devices  20.2 us (3%)
  between operations  15.1 us (2%)
    all_gather x4, waiting for transfers between devices, gather_plane(): stack = lax.all_gather(local, CHIPS, axis=0, tiled=False)  99.7 us
    ppermute x14, waiting for transfers between devices, swap(): return lax.ppermute(array_in, axis, [(0, 1), (1, 0)])  99.4 us
    psum x1, waiting for transfers between devices, shards(): out_sum, in_sum = lax.psum((out_part, in_part), 'dp')  81.8 us
    pallas_call x1, Pallas kernels, attend_back(): pl.pallas_call(functools.partial(backward_kernel, count // BLOCK), grid=(...  55.3 us
    unnamed x12, waiting for transfers between devices  47.8 us
    dot_general x5, matrix products, dot_nn(): return jnp.dot(left, right, preferred_element_type=jnp.float32)  47.4 us
    psum x1, waiting for transfers between devices, shards(): late_sum = lax.psum(scatter(late_stack), 'dp').astype(jnp.float32)  45.3 us
    pallas_call x1, Pallas kernels, attend(): pl.pallas_call(functools.partial(forward_kernel, count // BLOCK), grid=(w...  39.3 us
  transfers between devices with their start and end apart: 27, of which 13 were waited for; matrix products, arithmetic and copies ran while one was open for 24% of the time, Pallas kernels for 12%

profile of v2, /device:TPU:0, one launch (start us, length us, event | category | flops | bytes accessed | tf_op | source)
XLA Modules:
  0.0 766.9 jit_solution(6979739894938586790)
XLA Ops:
  11.3 3.0 collective-permute-start.3
  14.3 2.6 broadcast_select_fusion.10
  28.4 57.5 %collective-permute-done = bf16[1024,512]{1,0:T(8,128)(2,1)} collective-permute-done((bf16[1024,512]{1,0:T(8,128)(2,1)}, bf16[1024,512]{1,0:T(8,128)(2,1)}, u32[]{:S(2)}, u32[]{:S(2)}) %collective-permute-start) | collective-permute-done | bytes 1048608 | tf_op jit(solution)/shard_map/ppermute | solution.py:226
  88.0 2.2 collective-permute-start.1
  92.0 2.7 broadcast_select_fusion.9
  94.8 4.7 collective-permute-done.2
  101.1 2.7 fusion.9
  104.5 45.2 %all-gather.10.cloned.1.call-done = bf16[3072,512]{1,0:T(8,128)(2,1)} async-done(((bf16[768,512]{1,0:T(8,128)(2,1)}), bf16[3072,512]{1,0:T(8,128)(2,1)}) %all-gather.10.cloned.1.call-update) | async-done | bytes 3145744 | tf_op jit(solution)/shard_map/all_gather | solution.py:247
  150.4 4.9 multiply_convert_fusion.2
  160.3 53.7 %all-gather.8.cloned.1.call-done = bf16[4,1312,512]{2,1,0:T(8,128)(2,1)} async-done(((bf16[1,1312,512]{2,1,0:T(8,128)(2,1)}), bf16[4,1312,512]{2,1,0:T(8,128)(2,1)}) %all-gather.8.cloned.1.call-update) | async-done | bytes 5373968 | tf_op jit(solution)/shard_map/all_gather | solution.py:247
  218.6 3.0 maximum_maximum_fusion.1
  223.7 3.3 maximum_maximum_fusion
  227.1 39.3 %attend_forward.1 = (bf16[1024,1024]{1,0:T(8,128)(2,1)S(1)}, bf16[1152,1024]{1,0:T(8,128)(2,1)}, bf16[1152,1024]{1,0:T(8,128)(2,1)}, bf16[1024,1024]{1,0:T(8,128)(2,1)}) custom-call(bf16[1152,1024]{1,0:T(8,128)(2,1)} %get-tuple-element.50.normed_ref, bf16[4,3,256,1024]{3,2,1,0:T(8,128)(2,1)} %bitcast.163, bf16[4,3,256,1024]{3,2,1,0:T(8,128)(2,1)} %bitcast.164, ...), custom_call_target="tpu_custom_call" | custom-call | flops 9395240960 | bytes 18087936 | tf_op jit(solution)/shard_map/attend_forward/pallas_call | solution.py:149
  266.4 4.7 fusion.36
  273.6 2.9 slice_bitcast_fusion.1
  278.2 3.2 pad_maximum_fusion.2
  281.4 8.5 %fusion.50 = f32[1024,2624]{0,1:T(8,128)} fusion(bf16[1024,1024]{1,0:T(8,128)(2,1)S(1)} %multiply_convert_fusion.3, bf16[2624,1024]{1,0:T(8,128)(2,1)S(1)} %bitcast.176), kind=kOutput, calls=%fused_computation.205 | convolution fusion | flops 5502926848 | bytes 18219008 | tf_op jit(solution)/shard_map/dot_general | solution.py:30
  289.9 8.4 %fusion.49 = f32[1024,2624]{0,1:T(8,128)} fusion(bf16[1024,1024]{1,0:T(8,128)(2,1)S(1)} %multiply_convert_fusion.3, bf16[2624,1024]{1,0:T(8,128)(2,1)S(1)} %bitcast.179), kind=kOutput, calls=%fused_computation.204 | convolution fusion | flops 5502926848 | bytes 18219008 | tf_op jit(solution)/shard_map/dot_general | solution.py:30
  298.3 16.3 %multiply_convert_fusion = (bf16[1024,2624]{0,1:T(8,128)(2,1)S(1)}, bf16[1024,2624]{0,1:T(8,128)(2,1)}, bf16[1024,2624]{0,1:T(8,128)(2,1)}) fusion(f32[1024,2624]{0,1:T(8,128)} %fusion.49, f32[1024,2624]{0,1:T(8,128)} %fusion.50, bf16[2624,1024]{1,0:T(8,128)(2,1)S(1)} %bitcast.172, bf16[1024,512]{1,0:T(8,128)(2,1)S(1)} %copy-done.23, ...), kind=kOutput, calls=%fused_computation.7 | convolution fusion | flops 5550112768 | bytes 45088768 | tf_op jit(solution)/shard_map/dot_general | solution.py:30
  314.6 10.6 %convolution_convert_fusion = bf16[2624,1024]{1,0:T(8,128)(2,1)S(1)} fusion(bf16[1024,2624]{0,1:T(8,128)(2,1)} %get-tuple-element.25, bf16[1024,512]{1,0:T(8,128)(2,1)S(1)} %copy-done.23, bf16[1024,512]{1,0:T(8,128)(2,1)S(1)} %copy-done.22), kind=kOutput, calls=%fused_computation.14 | convolution fusion | flops 5509808128 | bytes 12845056 | tf_op jit(solution)/shard_map/dot_general | solution.py:36
  327.7 6.0 convolution_convert_fusion.3
  337.3 6.4 convolution_convert_fusion.2
  350.2 3.8 add_convert_fusion.3
  354.4 3.9 add_convert_fusion.2
  358.8 3.0 pad_maximum_fusion.3
  361.8 10.1 %fusion.51 = f32[1024,1024]{1,0:T(8,128)S(1)} fusion(bf16[1024,2624]{0,1:T(8,128)(2,1)} %get-tuple-element.28, bf16[2624,1024]{1,0:T(8,128)(2,1)} %bitcast.178), kind=kOutput, calls=%fused_computation.206 | convolution fusion | flops 5502926848 | bytes 14942208 | tf_op jit(solution)/shard_map/dot_general | solution.py:26
  371.9 11.0 %multiply_reduce_fusion = (bf16[1024]{0:T(1024)(128)(2,1)S(1)}, f32[1024]{0:T(1024)S(1)}, f32[1024]{0:T(1024)S(1)}, f32[1024,1024]{1,0:T(8,128)S(1)}) fusion(f32[1024,1024]{1,0:T(8,128)S(1)} %copy-done.6, f32[1024]{0:T(1024)S(1)} %add_rsqrt_fusion.1, f32[1024]{0:T(1024)S(1)} %broadcast_multiply_fusion.5, f32[1024]{0:T(1024)S(1)} %bitcast.201, ...), kind=kOutput, calls=%fused_computation.39 | convolution fusion | flops 5512360960 | bytes 23353344 | tf_op jit(solution)/shard_map/dot_general | solution.py:26
  384.8 3.7 convolution_convert_fusion.5.grad_ref
  388.5 55.3 %attend_backward.1 = (bf16[1024,1024]{1,0:T(8,128)(2,1)S(1)}, bf16[1152,1024]{1,0:T(8,128)(2,1)}, bf16[1152,1024]{1,0:T(8,128)(2,1)}) custom-call(bf16[1024,1024]{1,0:T(8,128)(2,1)} %copy-done.4, bf16[1152,1024]{1,0:T(8,128)(2,1)} %get-tuple-element.31.k_ref, bf16[1152,1024]{1,0:T(8,128)(2,1)} %get-tuple-element.32.v_ref, ...), custom_call_target="tpu_custom_call" | custom-call | flops 6442450944 | bytes 16515072 | tf_op jit(solution)/shard_map/attend_backward/pallas_call | solution.py:182
  448.7 3.3 collective-permute-start.12
  454.2 4.4 slice.360
  458.7 2.8 collective-permute-done.12
  463.4 2.7 pad_maximum_fusion.7
  476.5 11.1 %multiply_reduce_fusion.1 = (bf16[1024]{0:T(1024)(128)(2,1)S(1)}, f32[1024]{0:T(1024)S(1)}, f32[1024]{0:T(1024)S(1)}, f32[1024,1024]{1,0:T(8,128)}) fusion(f32[1152,1024]{1,0:T(8,128)S(1)} %bitcast.162, f32[1024]{0:T(1024)S(1)} %bitcast.198, bf16[1024,3072]{1,0:T(8,128)(2,1)} %slice_dynamic-update-slice_fusion, bf16[3072,1024]{1,0:T(8,128)(2,1)S(1)} %bitcast.168), kind=kOutput, calls=%fused_computation.40 | convolution fusion | flops 6448739328 | bytes 20985856 | tf_op jit(solution)/shard_map/dot_general | solution.py:26
  487.7 7.5 convolution_convert_fusion.1
  498.7 2.4 convolution_convert_fusion.4
  502.5 2.3 collective-permute-done.16
  509.7 13.4 %reduce-scatter.12.cloned.1.call-done = bf16[1,1312,512]{2,1,0:T(8,128)(2,1)} async-done(((bf16[4,1312,512]{2,1,0:T(8,128)(2,1)}), bf16[1,1312,512]{2,1,0:T(8,128)(2,1)}) %reduce-scatter.12.cloned.1.call-update) | async-done | bytes 1343504
  525.8 2.3 pad_maximum_fusion.6
  528.1 81.8 %all-reduce.11.cloned.1.call-done = (bf16[656,512]{1,0:T(8,128)(2,1)}, bf16[1312,512]{1,0:T(8,128)(2,1)}) async-done(((bf16[656,512]{1,0:T(8,128)(2,1)}, bf16[1312,512]{1,0:T(8,128)(2,1)}), (bf16[656,512]{1,0:T(8,128)(2,1)}, bf16[1312,512]{1,0:T(8,128)(2,1)})) %all-reduce.11.cloned.1.call-update) | async-done | bytes 2015248 | tf_op jit(solution)/shard_map/psum | solution.py:418
  610.0 10.5 %add_convert_fusion.5 = bf16[1024,1024]{1,0:T(8,128)(2,1)S(1)} fusion(f32[1024,1024]{1,0:T(8,128)} %copy-done.5, bf16[1024,2624]{0,1:T(8,128)(2,1)} %get-tuple-element.25, bf16[2624,1024]{1,0:T(8,128)(2,1)} %bitcast.169), kind=kOutput, calls=%fused_computation.45 | convolution fusion | flops 5505024000 | bytes 17039360 | tf_op jit(solution)/shard_map/dot_general | solution.py:26
  622.2 2.9 add_convert_fusion.4
  626.8 39.6 %collective-permute-done.9 = bf16[1024,512]{1,0:T(8,128)(2,1)S(1)} collective-permute-done((bf16[1024,512]{1,0:T(8,128)(2,1)S(1)}, bf16[1024,512]{1,0:T(8,128)(2,1)S(1)}, u32[]{:S(2)}, u32[]{:S(2)}) %collective-permute-start.9) | collective-permute-done | bytes 1048608 | tf_op jit(solution)/shard_map/ppermute | solution.py:226
  667.6 31.7 %reduce-scatter.14.cloned.1.call-done = bf16[1,1040,512]{2,1,0:T(8,128)(2,1)} async-done(((bf16[4,1040,512]{2,1,0:T(8,128)(2,1)}), bf16[1,1040,512]{2,1,0:T(8,128)(2,1)}) %reduce-scatter.14.cloned.1.call-update) | async-done | bytes 1064976
  699.3 2.7 pad_maximum_fusion.12
  703.4 2.6 maximum_convert_fusion
  709.1 45.3 %all-reduce.9.cloned.1.call-done = bf16[1040,512]{1,0:T(8,128)(2,1)} async-done(((bf16[1040,512]{1,0:T(8,128)(2,1)}), bf16[1040,512]{1,0:T(8,128)(2,1)}) %all-reduce.9.cloned.1.call-update) | async-done | bytes 1064976 | tf_op jit(solution)/shard_map/psum | solution.py:420
  757.6 2.5 slice.388
  (257 shorter events, 97.4 us)
Async XLA Ops:
  7.2 9.7 %copy-start.13 = (bf16[2048,512]{1,0:T(8,128)(2,1)S(1)}, bf16[2048,512]{1,0:T(8,128)(2,1)}, u32[]{:S(2)}) copy-start(bf16[2048,512]{1,0:T(8,128)(2,1)} %param.9) | copy-start | bytes 6291460
  7.2 93.4 %all-gather.14.cloned.1.call-start = ((), (), s32[]{:S(2)}) async-start(), calls=%async_computation.7 | async-start | bytes 3358720 | tf_op jit(solution)/shard_map/all_gather | solution.py:247
  7.9 96.6 %all-gather.12.cloned.1.call-start = ((), (), s32[]{:S(2)}) async-start(), calls=%async_computation.6 | async-start | bytes 1310720 | tf_op jit(solution)/shard_map/all_gather | solution.py:247
  8.7 141.1 %all-gather.10.cloned.1.call-start = ((), (), s32[]{:S(2)}) async-start(), calls=%async_computation.5 | async-start | bytes 3932160 | tf_op jit(solution)/shard_map/all_gather | solution.py:247
  8.7 11.3 %copy-start.40 = (s32[8192]{0:T(1024)S(1)}, s32[8192]{0:T(1024)}, u32[]{:S(2)}) copy-start(s32[8192]{0:T(1024)} %param.10) | copy-start | bytes 98308
  9.4 204.6 %all-gather.8.cloned.1.call-start = ((), (), s32[]{:S(2)}) async-start(), calls=%async_computation.3 | async-start | bytes 6717440 | tf_op jit(solution)/shard_map/all_gather | solution.py:247
  10.0 499.7 %reduce-scatter.10.cloned.1.call-start = ((), (), s32[]{:S(2)}) async-start(), calls=%async_computation.8 | async-start | bytes 3358720
  11.3 16.4 %collective-permute-start.3 = (f32[2,512]{1,0:T(2,128)}, f32[2,512]{1,0:T(2,128)}, u32[]{:S(2)}, u32[]{:S(2)}) collective-permute-start(f32[2,512]{1,0:T(2,128)} %pad_maximum_fusion.16), channel_id=1, source_target_pairs={{0,1},{1,0},{2,3},{3,2},{4,5},{5,4},{6,7},{7,6},{8,9},{9,8},{10,11... | collective-permute-start | bytes 12296 | tf_op jit(solution)/shard_map/ppermute | solution.py:226
  16.9 75.1 %collective-permute-start.7 = (bf16[1024,512]{1,0:T(8,128)(2,1)}, bf16[1024,512]{1,0:T(8,128)(2,1)}, u32[]{:S(2)}, u32[]{:S(2)}) collective-permute-start(bf16[1024,512]{1,0:T(8,128)(2,1)} %broadcast_select_fusion.10), channel_id=1, source_target_pairs={{0,1},{1,0},{2,3},{3,2},{4,5},{5,4},{6,7},{7,6},{8,9},{9,8},{10,11... | collective-permute-start | bytes 3145736 | tf_op jit(solution)/shard_map/ppermute | solution.py:226
  18.0 67.9 %collective-permute-start = (bf16[1024,512]{1,0:T(8,128)(2,1)}, bf16[1024,512]{1,0:T(8,128)(2,1)}, u32[]{:S(2)}, u32[]{:S(2)}) collective-permute-start(bf16[1024,512]{1,0:T(8,128)(2,1)} %broadcast_select_fusion.14), channel_id=1, source_target_pairs={{0,1},{1,0},{2,3},{3,2},{4,5},{5,4},{6,7},{7,6},{8,9},{9,8},{10,11... | collective-permute-start | bytes 3145736 | tf_op jit(solution)/shard_map/ppermute | solution.py:226
  24.6 202.5 %copy-start = (f32[1152,256]{1,0:T(8,128)}, f32[1152,256]{1,0:T(8,128)S(1)}, u32[]{:S(2)}) copy-start(f32[1152,256]{1,0:T(8,128)S(1)} %copy.53.cos_ref) | copy-start | bytes 3538948
  25.5 66.5 %copy-start.14 = (bf16[2048,512]{1,0:T(8,128)(2,1)S(1)}, bf16[2048,512]{1,0:T(8,128)(2,1)}, u32[]{:S(2)}) copy-start(bf16[2048,512]{1,0:T(8,128)(2,1)} %param.17) | copy-start | bytes 6291460
  28.4 122.0 %copy-start.38 = (f32[1,1024]{1,0:T(1,128)}, f32[1,1024]{1,0:T(1,128)S(1)}, u32[]{:S(2)}) copy-start(f32[1,1024]{1,0:T(1,128)S(1)} %get-tuple-element.130) | copy-start | bytes 12292
  87.9 12.6 %copy-start.7 = (bf16[1024,512]{1,0:T(8,128)(2,1)}, bf16[1024,512]{1,0:T(8,128)(2,1)S(1)}, u32[]{:S(2)}) copy-start(bf16[1024,512]{1,0:T(8,128)(2,1)S(1)} %get-tuple-element.82) | copy-start | bytes 3145732
  88.0 6.8 collective-permute-start.1
  90.2 9.3 %collective-permute-start.2 = (bf16[64,1024]{1,0:T(8,128)(2,1)S(1)}, bf16[64,1024]{1,0:T(8,128)(2,1)S(1)}, u32[]{:S(2)}, u32[]{:S(2)}) collective-permute-start(bf16[64,1024]{1,0:T(8,128)(2,1)S(1)} %get-tuple-element.100), channel_id=1, source_target_pairs={{1,0},{2,1},{3,2},{4,3},{5,4},{6,5},{7,6},{9,8},{10,9},{11,10},{12... | collective-permute-start | bytes 393224 | tf_op jit(solution)/shard_map/ppermute | solution.py:323
  100.6 115.5 %collective-permute-start.8 = (bf16[4,656,512]{2,1,0:T(8,128)(2,1)}, bf16[4,656,512]{2,1,0:T(8,128)(2,1)}, u32[]{:S(2)}, u32[]{:S(2)}) collective-permute-start(bf16[4,656,512]{2,1,0:T(8,128)(2,1)} %bitcast.184), channel_id=1, source_target_pairs={{0,2},{2,0},{1,3},{3,1},{4,6},{6,4},{5,7},{7,5},{8,10},{10,8},{9,1... | collective-permute-start | bytes 8060936 | tf_op jit(solution)/shard_map/ppermute | solution.py:226
  104.5 51.0 %collective-permute-start.5 = (bf16[4,256,512]{2,1,0:T(8,128)(2,1)}, bf16[4,256,512]{2,1,0:T(8,128)(2,1)}, u32[]{:S(2)}, u32[]{:S(2)}) collective-permute-start(bf16[4,256,512]{2,1,0:T(8,128)(2,1)} %bitcast.193), channel_id=1, source_target_pairs={{0,2},{2,0},{1,3},{3,1},{4,6},{6,4},{5,7},{7,5},{8,10},{10,8},{9,1... | collective-permute-start | bytes 3145736 | tf_op jit(solution)/shard_map/ppermute | solution.py:226
  149.7 71.9 %collective-permute-start.4 = (bf16[4,768,512]{2,1,0:T(8,128)(2,1)}, bf16[4,768,512]{2,1,0:T(8,128)(2,1)}, u32[]{:S(2)}, u32[]{:S(2)}) collective-permute-start(bf16[4,768,512]{2,1,0:T(8,128)(2,1)} %bitcast.182), channel_id=1, source_target_pairs={{0,2},{2,0},{1,3},{3,1},{4,6},{6,4},{5,7},{7,5},{8,10},{10,8},{9,1... | collective-permute-start | bytes 9437192 | tf_op jit(solution)/shard_map/ppermute | solution.py:226
  214.0 59.6 %collective-permute-start.6 = (bf16[4,1312,512]{2,1,0:T(8,128)(2,1)}, bf16[4,1312,512]{2,1,0:T(8,128)(2,1)}, u32[]{:S(2)}, u32[]{:S(2)}) collective-permute-start(bf16[4,1312,512]{2,1,0:T(8,128)(2,1)} %all-gather.8.cloned.1.call-done), channel_id=1, source_target_pairs={{0,2},{2,0},{1,3},{3,1},{4,6},{6,4},{5,7},{7,5},{8,10},{10,8},{9,1... | collective-permute-start | bytes 16121864 | tf_op jit(solution)/shard_map/ppermute | solution.py:226
  223.7 49.5 %slice-start.6 = ((s8[5373952]{0:T(1024)(128)(4,1)}), s8[1179648]{0:T(1024)(128)(4,1)S(1)}, s32[]{:S(2)}) async-start(s8[5373952]{0:T(1024)(128)(4,1)} %bitcast.173), calls=%async_computation.18 | async-start | bytes 2359296
  227.1 39.4 %copy-start.8 = (bf16[1024,512]{1,0:T(8,128)(2,1)S(1)}, bf16[1024,512]{1,0:T(8,128)(2,1)}, u32[]{:S(2)}) copy-start(bf16[1024,512]{1,0:T(8,128)(2,1)} %copy-done.7) | copy-start | bytes 3145732
  227.1 39.4 %copy-start.28 = (bf16[4,256,1024]{2,1,0:T(8,128)(2,1)S(1)}, bf16[4,256,1024]{2,1,0:T(8,128)(2,1)}, u32[]{:S(2)}) copy-start(bf16[4,256,1024]{2,1,0:T(8,128)(2,1)} %maximum_maximum_fusion.2) | copy-start | bytes 6291460
  227.1 46.1 %slice-start.7 = ((s8[5373952]{0:T(1024)(128)(4,1)}), s8[4194304]{0:T(1024)(128)(4,1)S(1)}, s32[]{:S(2)}) async-start(s8[5373952]{0:T(1024)(128)(4,1)} %bitcast.173), calls=%async_computation.19 | async-start | bytes 8388608
  281.4 16.9 %slice-start.4 = ((s8[5373952]{0:T(1024)(128)(4,1)}), s8[4194304]{0:T(1024)(128)(4,1)S(1)}, s32[]{:S(2)}) async-start(s8[5373952]{0:T(1024)(128)(4,1)} %bitcast.170), calls=%async_computation.16 | async-start | bytes 8388608
  314.6 22.7 %copy-start.43 = (bf16[1024,2624]{0,1:T(8,128)(2,1)}, bf16[1024,2624]{0,1:T(8,128)(2,1)S(1)}, u32[]{:S(2)}) copy-start(bf16[1024,2624]{0,1:T(8,128)(2,1)S(1)} %get-tuple-element.29) | copy-start | bytes 16121860
  325.5 21.4 %collective-permute-start.17 = (bf16[1312,1024]{1,0:T(8,128)(2,1)S(1)}, bf16[1312,1024]{1,0:T(8,128)(2,1)S(1)}, u32[]{:S(2)}, u32[]{:S(2)}) collective-permute-start(bf16[1312,1024]{1,0:T(8,128)(2,1)S(1)} %split.125), channel_id=1, source_target_pairs={{0,2},{2,0},{1,3},{3,1},{4,6},{6,4},{5,7},{7,5},{8,10},{10,8},{9,1... | collective-permute-start | bytes 8060936 | tf_op jit(solution)/shard_map/ppermute | solution.py:226
  336.8 13.4 %collective-permute-start.10 = (bf16[1312,1024]{1,0:T(8,128)(2,1)}, bf16[1312,1024]{1,0:T(8,128)(2,1)}, u32[]{:S(2)}, u32[]{:S(2)}) collective-permute-start(bf16[1312,1024]{1,0:T(8,128)(2,1)} %split.107), channel_id=1, source_target_pairs={{0,2},{2,0},{1,3},{3,1},{4,6},{6,4},{5,7},{7,5},{8,10},{10,8},{9,1... | collective-permute-start | bytes 8060936 | tf_op jit(solution)/shard_map/ppermute | solution.py:226
  345.7 8.7 %collective-permute-start.11 = (bf16[1312,1024]{1,0:T(8,128)(2,1)}, bf16[1312,1024]{1,0:T(8,128)(2,1)}, u32[]{:S(2)}, u32[]{:S(2)}) collective-permute-start(bf16[1312,1024]{1,0:T(8,128)(2,1)} %split.109), channel_id=1, source_target_pairs={{0,2},{2,0},{1,3},{3,1},{4,6},{6,4},{5,7},{7,5},{8,10},{10,8},{9,1... | collective-permute-start | bytes 8060936 | tf_op jit(solution)/shard_map/ppermute | solution.py:226
  350.2 173.0 %reduce-scatter.12.cloned.1.call-start = ((), (), s32[]{:S(2)}) async-start(), calls=%async_computation.9 | async-start | bytes 6717440
  361.8 10.1 %copy-start.6 = (f32[1024,1024]{1,0:T(8,128)S(1)}, f32[1024,1024]{1,0:T(8,128)}, u32[]{:S(2)}) copy-start(f32[1024,1024]{1,0:T(8,128)} %copy-done.5) | copy-start | bytes 12582916
  448.7 12.8 %collective-permute-start.12 = (bf16[64,2048]{1,0:T(8,128)(2,1)S(1)}, bf16[64,2048]{1,0:T(8,128)(2,1)S(1)}, u32[]{:S(2)}, u32[]{:S(2)}) collective-permute-start(bf16[64,2048]{1,0:T(8,128)(2,1)S(1)} %get-tuple-element.63), channel_id=1, source_target_pairs={{0,1},{1,2},{2,3},{3,4},{4,5},{5,6},{6,7},{8,9},{9,10},{10,11},{11... | collective-permute-start | bytes 786440 | tf_op jit(solution)/shard_map/ppermute | solution.py:386
  452.0 10.1 %collective-permute-start.13 = (bf16[64,2048]{1,0:T(8,128)(2,1)S(1)}, bf16[64,2048]{1,0:T(8,128)(2,1)S(1)}, u32[]{:S(2)}, u32[]{:S(2)}) collective-permute-start(bf16[64,2048]{1,0:T(8,128)(2,1)S(1)} %get-tuple-element.64), channel_id=1, source_target_pairs={{1,0},{2,1},{3,2},{4,3},{5,4},{6,5},{7,6},{9,8},{10,9},{11,10},{12... | collective-permute-start | bytes 786440 | tf_op jit(solution)/shard_map/ppermute | solution.py:387
  458.6 151.2 %all-reduce.11.cloned.1.call-start = ((), (), s32[]{:S(2)}) async-start(), calls=%async_computation.11 | async-start | bytes 4030464 | tf_op jit(solution)/shard_map/psum | solution.py:418
  463.4 13.1 %slice-start = ((s8[4718592]{0:T(1024)(128)(4,1)}), s8[4194304]{0:T(1024)(128)(4,1)S(1)}, s32[]{:S(2)}) async-start(s8[4718592]{0:T(1024)(128)(4,1)} %bitcast.161), calls=%async_computation.12 | async-start | bytes 8388608
  463.4 13.1 %slice-start.2 = ((s8[6291456]{0:T(1024)(128)(4,1)}), s8[4194304]{0:T(1024)(128)(4,1)S(1)}, s32[]{:S(2)}) async-start(s8[6291456]{0:T(1024)(128)(4,1)} %bitcast.166), calls=%async_computation.14 | async-start | bytes 8388608
  467.1 9.4 %slice-start.3 = ((s8[6291456]{0:T(1024)(128)(4,1)}), s8[2097152]{0:T(1024)(128)(4,1)S(1)}, s32[]{:S(2)}) async-start(s8[6291456]{0:T(1024)(128)(4,1)} %bitcast.166), calls=%async_computation.15 | async-start | bytes 4194304
  476.5 11.1 %copy-start.27 = (bf16[1152,1024]{1,0:T(8,128)(2,1)S(1)}, bf16[1152,1024]{1,0:T(8,128)(2,1)}, u32[]{:S(2)}) copy-start(bf16[1152,1024]{1,0:T(8,128)(2,1)} %get-tuple-element.50.normed_ref) | copy-start | bytes 7077892
  476.5 11.1 %copy-start.37 = (bf16[1024,3072]{1,0:T(8,128)(2,1)S(1)}, bf16[1024,3072]{1,0:T(8,128)(2,1)}, u32[]{:S(2)}) copy-start(bf16[1024,3072]{1,0:T(8,128)(2,1)} %slice_dynamic-update-slice_fusion) | copy-start | bytes 18874372
  496.2 9.9 %collective-permute-start.15 = (bf16[1552,1024]{1,0:T(8,128)(2,1)S(1)}, bf16[1552,1024]{1,0:T(8,128)(2,1)S(1)}, u32[]{:S(2)}, u32[]{:S(2)}) collective-permute-start(bf16[1552,1024]{1,0:T(8,128)(2,1)S(1)} %pad_maximum_fusion.4), channel_id=1, source_target_pairs={{0,2},{2,0},{1,3},{3,1},{4,6},{6,4},{5,7},{7,5},{8,10},{10,8},{9,1... | collective-permute-start | bytes 9535496 | tf_op jit(solution)/shard_map/ppermute | solution.py:226
  501.3 3.6 collective-permute-start.16
  523.2 176.1 %reduce-scatter.14.cloned.1.call-start = ((), (), s32[]{:S(2)}) async-start(), calls=%async_computation.10 | async-start | bytes 5324800
  528.1 81.8 %copy-start.36 = (f32[1152]{0:T(1024)S(1)}, f32[1152]{0:T(1024)}, u32[]{:S(2)}) copy-start(f32[1152]{0:T(1024)} %copy-done.35) | copy-start | bytes 13828
  609.9 144.5 %all-reduce.9.cloned.1.call-start = ((), (), s32[]{:S(2)}) async-start(), calls=%async_computation.4 | async-start | bytes 2129920 | tf_op jit(solution)/shard_map/psum | solution.py:420
  610.0 12.2 %copy-start.11 = (f32[1024,1024]{1,0:T(8,128)S(1)}, f32[1024,1024]{1,0:T(8,128)}, u32[]{:S(2)}) copy-start(f32[1024,1024]{1,0:T(8,128)} %copy-done.9) | copy-start | bytes 12582916
  610.0 12.2 %copy-start.24 = (f32[1024,1024]{1,0:T(8,128)S(1)}, f32[1024,1024]{1,0:T(8,128)}, u32[]{:S(2)}) copy-start(f32[1024,1024]{1,0:T(8,128)} %get-tuple-element.134) | copy-start | bytes 12582916
  620.6 45.7 %collective-permute-start.9 = (bf16[1024,512]{1,0:T(8,128)(2,1)S(1)}, bf16[1024,512]{1,0:T(8,128)(2,1)S(1)}, u32[]{:S(2)}, u32[]{:S(2)}) collective-permute-start(bf16[1024,512]{1,0:T(8,128)(2,1)S(1)} %broadcast_select_fusion.6), channel_id=1, source_target_pairs={{0,1},{1,0},{2,3},{3,2},{4,5},{5,4},{6,7},{7,6},{8,9},{9,8},{10,11... | collective-permute-start | bytes 3145736 | tf_op jit(solution)/shard_map/ppermute | solution.py:226
  626.2 75.7 %collective-permute-start.14 = (bf16[1024,512]{1,0:T(8,128)(2,1)}, bf16[1024,512]{1,0:T(8,128)(2,1)}, u32[]{:S(2)}, u32[]{:S(2)}) collective-permute-start(bf16[1024,512]{1,0:T(8,128)(2,1)} %broadcast_select_fusion.2), channel_id=1, source_target_pairs={{0,1},{1,0},{2,3},{3,2},{4,5},{5,4},{6,7},{7,6},{8,9},{9,8},{10,11... | collective-permute-start | bytes 3145736 | tf_op jit(solution)/shard_map/ppermute | solution.py:226
  (33 other events, 133.7 us)
Sparse Core Ops, SparseCore 0:
  9.9 64.7 all-gather.13
  76.5 27.9 all-gather.11
  106.3 43.3 all-gather.9
  151.4 62.5 all-gather.7
  350.3 40.1 reduce-scatter.9
  458.7 64.3 reduce-scatter.11
  525.6 84.1 all-reduce.10
  613.1 86.0 reduce-scatter.13
  701.8 52.6 all-reduce.8
